TPU v7x, 256 devices: a whole 4x4x8 slice. The times are simulated.
256 devices in a mesh: row: 8 (over x, core), col: 32 (over y, z).
Axes of the slice: x: 4, y: 4, z: 8, core: 2. Of those that a mesh axis runs over, the one named last changes fastest.
Arguments:
- blocks: float32 [2048, 8, 128, 128], P(('row', 'col')), may hold values from -2 to 2
- prolong: float32 [2048, 128, 128], P(('row', 'col')), may hold values from -0.5 to 0.5
- counts: int32 [2048], P(('row', 'col')), may hold values from 1 to 8
- columns: int32 [2048, 8], P(('row', 'col')), may hold values from 0 to 255, as said below
- aggregates: int32 [2048], P(('row', 'col')), may hold values from 0 to 1
Outputs:
- coarse_operator: float32 [512, 64, 128, 128], P(('row', 'col'))
Inputs may be any that keep to these rules, and one draw needn't show every extreme that they name: Over all slots of the 8 rows of one device, the columns that fall among the rows of any one device of the slab (columns // 8 equal) take at most 2 distinct values; every device reaches 2 for some such device.
All inputs are finite; a program needn't handle non-finite values.
Results may differ from a plain program's by a relative error of at most 0.0003.
Values sent between devices are 32-bit elements; how exact they have to be, the bound alone decides.
No kernel may reach another device: no remote copies, remote signals or barrier semaphores. Data moves between devices by JAX's collectives and lax.ppermute only.
A program may use at most 64 MiB of HBM per device.

v0:
```python
import functools

import jax
import jax.numpy as jnp
from jax import lax
from jax.sharding import Mesh
from jax.sharding import PartitionSpec as P

AGD = 2
CAP = 2
COL = ("col_0", "col_1")
ROW_COL = ("row_0", "row_1", "col_0", "col_1")


def in_order(tiles, dim):
    dims = list(tiles.shape[1:])
    dims[dim] *= tiles.shape[0]
    return jnp.moveaxis(tiles, 0, dim).reshape(dims)


def from_everyone(shard, axis):
    copies = jnp.broadcast_to(shard, (lax.axis_size(axis), *shard.shape))
    return lax.all_to_all(copies, axis, split_axis=0, concat_axis=0, tiled=True)


def collect(shard, axis, dim):
    return in_order(from_everyone(shard, axis), dim)


def one_axis_at_a_time(shard, axes):
    return functools.reduce(lax.pmax, axes, shard)


def per_device(blocks, prolong, counts, columns, aggregates):
    rows_here, slots = columns.shape
    tile = blocks.shape[-1]
    peers = lax.axis_size(COL)
    wide = AGD * peers
    high = lax.Precision.HIGHEST
    flat_cols = columns.reshape(-1)
    slab_agg = collect(aggregates, COL, 0)
    col_agg = jnp.take(slab_agg, columns, axis=0)
    coarse_col = columns // rows_here * AGD + col_agg
    every_block = jnp.arange(rows_here * peers, dtype=jnp.int32)
    wanted = jnp.any(flat_cols[:, None] == every_block[None, :], axis=0)
    wanted = wanted.reshape(peers, rows_here).astype(jnp.int32)
    rank = jnp.cumsum(wanted, axis=1) - 1
    places = jnp.arange(CAP, dtype=jnp.int32)
    local_ids = jnp.arange(rows_here, dtype=jnp.int32)
    match = (wanted[:, :, None] > 0) & (rank[:, :, None] == places[None, None, :])
    valid = jnp.any(match, axis=1)
    chosen = jnp.sum(jnp.where(match, local_ids[None, :, None], 0), axis=1)
    requests = jnp.where(valid, chosen, -1)
    asked = lax.all_to_all(requests, COL, split_axis=0, concat_axis=0, tiled=True)
    found = jnp.take(prolong, jnp.clip(asked, 0, rows_here - 1).reshape(-1), axis=0)
    found = jnp.where((asked.reshape(-1) >= 0)[:, None, None], found, 0.0)
    found = found.reshape(peers, CAP, tile, tile)
    replies = lax.all_to_all(found, COL, split_axis=0, concat_axis=0, tiled=True)
    replies = replies.reshape(peers * CAP, tile, tile)
    owner = flat_cols // rows_here
    within = flat_cols % rows_here
    slot_rank = rank.reshape(-1)[owner * rows_here + within]
    picked = jnp.take(replies, owner * CAP + slot_rank, axis=0)
    picked = picked.reshape(rows_here, slots, tile, tile)
    inner = jnp.einsum("bxw,bkxy->bkwy", prolong, blocks, precision=high)
    terms = jnp.einsum("bkwy,bkyz->bkwz", inner, picked, precision=high)
    live = (jnp.arange(slots, dtype=jnp.int32)[None, :] < counts[:, None]).astype(jnp.float32)
    col_hot = (coarse_col[:, :, None] == jnp.arange(wide, dtype=jnp.int32)[None, None, :]).astype(
        jnp.float32
    ) * live[:, :, None]
    row_hot = (aggregates[:, None] == jnp.arange(AGD, dtype=jnp.int32)[None, :]).astype(jnp.float32)
    weights = (row_hot[:, None, :, None] * col_hot[:, :, None, :]).reshape(
        rows_here * slots, AGD * wide
    )
    flat_terms = terms.reshape(rows_here * slots, tile * tile)
    galerkin = jnp.dot(weights.T, flat_terms, precision=high).reshape(AGD, wide, tile, tile)
    local_most = jnp.max(jnp.sum(jnp.abs(galerkin), axis=(1, 3)))
    bound = one_axis_at_a_time(local_most, ROW_COL)
    return galerkin / (bound + 1e-06)


def solution(mesh):
    torus = Mesh(mesh.devices.reshape(4, 2, 4, 8), ("row_0", "row_1", "col_0", "col_1"))
    placed = (
        P(ROW_COL, None, None, None),
        P(ROW_COL, None, None),
        P(ROW_COL),
        P(ROW_COL, None),
        P(ROW_COL),
    )
    return jax.shard_map(
        per_device,
        mesh=torus,
        in_specs=placed,
        out_specs=P(ROW_COL, None, None, None),
        check_vma=False,
    )
```

profile of v0, /device:TPU:8, one launch (start us, length us, event | category | flops | bytes accessed | tf_op | source)
XLA Modules:
  0.0 219.1 jit_solution(3474505113296030282)
XLA Ops:
  0.0 0.0 copy-start
  0.0 0.8 reshape.314
  0.8 0.1 fusion.11
  0.9 0.1 reshape.318
  1.0 0.1 copy.39
  1.1 0.2 reduce_window_sum.11
  1.3 0.1 copy.40
  1.4 0.1 copy.41
  1.5 20.1 %all_to_all.17 = s32[32,1,2]{2,1,0:T(1,128)S(1)} all-to-all(s32[32,1,2]{2,1,0:T(1,128)S(1)} %copy.41), channel_id=1, replica_groups=mesh['row_0'=4,'row_1'=2,'col_0'=4,'col_1'=8] {'col_0','col_1'}, dimensions={0} | all-to-all | bytes 512 | tf_op jit(solution)/shard_map/all_to_all | solution.py:54
  21.6 1.3 broadcast_in_dim.75
  22.9 5.0 %all-to-all-start = ((s32[32,1,8]{2,1,0:T(1,128)}), s32[32,1,8]{2,1,0:T(1,128)S(1)}, u32[]{:S(2)}, u32[]{:S(2)}) async-start(s32[32,1,8]{2,1,0:T(1,128)} %broadcast_in_dim.75), calls=%async_computation | async-start | bytes 32768 | tf_op jit(solution)/shard_map/all_to_all | solution.py:23
  27.8 0.1 copy.42
  28.0 0.1 copy.43
  28.1 0.1 copy.45
  28.2 0.1 copy.46
  28.3 0.1 min.12
  28.4 0.0 copy-done
  28.4 2.8 %gather_fusion.2 = f32[64,128,128]{2,1,0:T(8,128)} fusion(f32[8,128,128]{2,1,0:T(8,128)S(1)} %copy-done, s32[1024]{0:T(1024)S(1)} %pad_clamp_fusion.1), kind=kCustom, calls=%fused_computation.2 | custom fusion | bytes 8388864 | tf_op jit(solution)/shard_map/jit(_take)/gather | solution.py:55
  31.2 4.6 %select_select_fusion = f32[32,2,128,128]{3,2,1,0:T(8,128)} fusion(f32[32,2,128,128]{3,2,1,0:T(8,128)} %bitcast.58, pred[32,2]{1,0:T(8,128)(4,1)S(1)} %copy.45, pred[32,2]{1,0:T(8,128)(4,1)S(1)} %copy.43), kind=kLoop, calls=%fused_computation.12 | loop fusion | flops 2097152 | bytes 8388736 | tf_op jit(solution)/shard_map/jit(_where)/select_n | solution.py:56
  35.9 0.0 copy-start.1
  35.9 0.0 copy-start.2
  35.9 0.0 copy-start.3
  35.9 0.6 all-to-all-done
  36.5 9.4 %all-to-all-start.2 = ((f32[32,2,128,128]{3,2,1,0:T(8,128)}), f32[32,2,128,128]{3,2,1,0:T(8,128)}, u32[]{:S(2)}, u32[]{:S(2)}) async-start(f32[32,2,128,128]{3,2,1,0:T(8,128)} %select_select_fusion), calls=%async_computation.2 | async-start | bytes 8388608 | tf_op jit(solution)/shard_map/all_to_all | solution.py:58
  45.9 0.0 copy-done.1
  46.0 0.1 reshape.315
  46.0 0.1 sub.20
  46.1 0.1 reshape.321
  46.2 0.8 gather_fusion.1
  47.0 0.1 gather.25
  47.2 0.0 copy-done.2
  47.2 0.1 fusion.17
  47.2 0.0 copy-done.3
  47.2 0.1 fusion.19
  47.3 8.0 %fusion.9 = f32[8,8,128,128]{2,3,1,0:T(8,128)} fusion(f32[8,8,128,128]{3,2,1,0:T(8,128)} %param.5, f32[8,128,128]{2,1,0:T(8,128)S(1)} %copy-done), kind=kOutput, calls=%fused_computation.16 | convolution fusion | flops 1610612736 | bytes 8912896 | tf_op jit(solution)/shard_map/bxw,bkxy->bkwy/dot_general | solution.py:65
  55.4 0.5 broadcast.393
  55.8 0.6 reduce.3
  56.5 0.1 reshape.313
  56.5 0.8 gather_fusion
  57.3 0.1 reshape.320
  57.4 0.1 fusion.12
  57.5 0.1 broadcast_multiply_fusion
  57.6 0.1 mul.65
  57.7 0.1 copy.55
  57.8 80.9 %all-to-all-done.2 = f32[32,2,128,128]{3,2,1,0:T(8,128)} async-done(((f32[32,2,128,128]{3,2,1,0:T(8,128)}), f32[32,2,128,128]{3,2,1,0:T(8,128)}, u32[]{:S(2)}, u32[]{:S(2)}) %all-to-all-start.2) | async-done | bytes 4194336 | tf_op jit(solution)/shard_map/all_to_all | solution.py:58
  138.7 5.0 %gather_fusion.3 = f32[64,128,128]{2,1,0:T(8,128)} fusion(f32[64,128,128]{2,1,0:T(8,128)} %bitcast.12, s32[1024]{0:T(1024)S(1)} %pad_clamp_fusion), kind=kCustom, calls=%fused_computation.3 | custom fusion | bytes 8388864 | tf_op jit(solution)/shard_map/jit(_take)/gather | solution.py:63
  143.7 6.8 %fusion.4 = f32[8,8,128,128]{3,2,1,0:T(8,128)S(1)} fusion(f32[8,8,128,128]{2,3,1,0:T(8,128)} %fusion.9, f32[8,8,128,128]{3,2,1,0:T(8,128)} %bitcast.57, pred[8,8]{1,0:T(8,128)(4,1)S(1)} %compare_and_fusion), kind=kOutput, calls=%fused_computation.13 | convolution fusion | flops 1611661312 | bytes 12582976 | tf_op jit(solution)/shard_map/bkwy,bkyz->bkwz/dot_general | solution.py:66
  150.4 13.8 %abs_reduce_fusion = (f32[2,128]{1,0:T(2,128)S(1)}, f32[2,64,128,128]{3,1,2,0:T(8,128)}) fusion(f32[2,64,64,1]{2,1,3,0:T(8,128)S(1)} %bitcast.59, f32[8,8,128,128]{3,2,1,0:T(8,128)S(1)} %fusion.4), kind=kOutput, calls=%fused_computation.4 | convolution fusion | flops 1614806784 | bytes 12616704 | tf_op jit(solution)/shard_map/dot_general | solution.py:76
  164.2 0.7 reduce_max.9
  164.9 11.2 %pmax.28 = f32[]{:T(128)} all-reduce(f32[]{:T(128)} %reduce_max.9), channel_id=1, replica_groups=mesh['row_0'=4,'row_1'=2,'col_0'=4,'col_1'=8] {'row_0'}, use_global_device_ids=true, to_apply=%region_6.7 | all-reduce | flops 1 | bytes 8 | tf_op jit(solution)/shard_map/pmax | solution.py:31
  176.1 3.2 %pmax.29 = f32[]{:T(128)} all-reduce(f32[]{:T(128)} %pmax.28), channel_id=1, replica_groups=mesh['row_0'=4,'row_1'=2,'col_0'=4,'col_1'=8] {'row_1'}, use_global_device_ids=true, to_apply=%region_7.8 | all-reduce | flops 1 | bytes 8 | tf_op jit(solution)/shard_map/pmax | solution.py:31
  179.3 11.4 %pmax.30 = f32[]{:T(128)} all-reduce(f32[]{:T(128)} %pmax.29), channel_id=1, replica_groups=mesh['row_0'=4,'row_1'=2,'col_0'=4,'col_1'=8] {'col_0'}, use_global_device_ids=true, to_apply=%region_8.9 | all-reduce | flops 1 | bytes 8 | tf_op jit(solution)/shard_map/pmax | solution.py:31
  190.7 15.1 %pmax.31 = f32[]{:T(128)} all-reduce(f32[]{:T(128)} %pmax.30), channel_id=1, replica_groups=mesh['row_0'=4,'row_1'=2,'col_0'=4,'col_1'=8] {'col_1'}, use_global_device_ids=true, to_apply=%region_9.10 | all-reduce | flops 1 | bytes 8 | tf_op jit(solution)/shard_map/pmax | solution.py:31
  206.5 4.4 %broadcast_divide_fusion = f32[2,64,128,128]{3,1,2,0:T(8,128)S(1)} fusion(f32[2,64,128,128]{3,1,2,0:T(8,128)} %get-tuple-element.8, f32[]{:T(128)S(6)} %add.143), kind=kLoop, calls=%fused_computation.9 | loop fusion | flops 2097152 | bytes 16777220 | tf_op jit(solution)/shard_map/div | solution.py:79
  210.8 8.3 %copy.50 = f32[2,64,128,128]{3,2,1,0:T(8,128)} copy(f32[2,64,128,128]{3,1,2,0:T(8,128)S(1)} %broadcast_divide_fusion) | data formatting | bytes 16777216 | tf_op jit(solution)/shard_map/div | solution.py:79
  (19 shorter events, 0.2 us)
Async XLA Ops:
  0.0 28.4 %copy-start = (f32[8,128,128]{2,1,0:T(8,128)S(1)}, f32[8,128,128]{2,1,0:T(8,128)}, u32[]{:S(2)}) copy-start(f32[8,128,128]{2,1,0:T(8,128)} %param.6) | copy-start | bytes 1572868
  22.9 13.6 %all-to-all-start = ((s32[32,1,8]{2,1,0:T(1,128)}), s32[32,1,8]{2,1,0:T(1,128)S(1)}, u32[]{:S(2)}, u32[]{:S(2)}) async-start(s32[32,1,8]{2,1,0:T(1,128)} %broadcast_in_dim.75), calls=%async_computation | async-start | bytes 32768 | tf_op jit(solution)/shard_map/all_to_all | solution.py:23
  35.9 10.1 %copy-start.1 = (s32[8,8]{1,0:T(8,128)S(1)}, s32[8,8]{1,0:T(8,128)}, u32[]{:S(2)}) copy-start(s32[8,8]{1,0:T(8,128)} %param.8) | copy-start | bytes 772
  35.9 11.3 %copy-start.2 = (s32[8]{0:T(128)S(1)}, s32[8]{0:T(128)}, u32[]{:S(2)}) copy-start(s32[8]{0:T(128)} %param.9) | copy-start | bytes 100
  35.9 11.4 %copy-start.3 = (s32[8]{0:T(128)S(1)}, s32[8]{0:T(128)}, u32[]{:S(2)}) copy-start(s32[8]{0:T(128)} %param.7) | copy-start | bytes 100
  36.5 102.2 %all-to-all-start.2 = ((f32[32,2,128,128]{3,2,1,0:T(8,128)}), f32[32,2,128,128]{3,2,1,0:T(8,128)}, u32[]{:S(2)}, u32[]{:S(2)}) async-start(f32[32,2,128,128]{3,2,1,0:T(8,128)} %select_select_fusion), calls=%async_computation.2 | async-start | bytes 8388608 | tf_op jit(solution)/shard_map/all_to_all | solution.py:58
where the time goes:
time: 220 us; the launch traced here: 219 us
  waiting for transfers between devices  81.5 us (37%)
  blocking collectives  61 us (28%)
  matrix products  28.6 us (13%)
  local copies, waits for them, and re-layouts  21.7 us (10%)
  starting transfers between devices  14.4 us (7%)
  other arithmetic  11 us (5%)
    all_to_all x1, waiting for transfers between devices, per_device(): lax.all_to_all(found, COL, split_axis=0, concat_axis=0, tiled=True)  80.9 us
    pmax x4, blocking collectives, one_axis_at_a_time(): return functools.reduce(lax.pmax, axes, shard)  40.9 us
    all_to_all x1, blocking collectives, per_device(): lax.all_to_all(requests, COL, split_axis=0, concat_axis=0, tiled=True)  20.1 us
    dot_general x1, matrix products, per_device(): jnp.dot(weights.T, flat_terms, precision=high)  13.8 us
    all_to_all x1, starting transfers between devices, per_device(): lax.all_to_all(found, COL, split_axis=0, concat_axis=0, tiled=True)  9.41 us
    div x1, local copies, waits for them, and re-layouts, per_device(): return galerkin / (bound + 1e-06)  8.25 us
    dot_general x1, matrix products, per_device(): inner = jnp.einsum('bxw,bkxy->bkwy', prolong, blocks, precision=high)  8.02 us
    dot_general x1, matrix products, per_device(): terms = jnp.einsum('bkwy,bkyz->bkwz', inner, picked, precision=high)  6.77 us
  transfers between devices with their start and end apart: 2, of which 2 were waited for; matrix products, arithmetic and copies ran while one was open for 9% of the time, Pallas kernels for 0%

commit v1 on v0

v1 whole, which is shorter than its diff:
```python
import functools

import jax
import jax.numpy as jnp
from jax import lax
from jax.experimental import pallas as pl
from jax.experimental.pallas import tpu as pltpu
from jax.sharding import Mesh
from jax.sharding import PartitionSpec as P

AGD = 2
CAP = 2
COL = ("col_0", "col_1")
ROW_COL = ("row_0", "row_1", "col_0", "col_1")
ANY = pl.BlockSpec(memory_space=pl.ANY)
SMEM = pl.BlockSpec(memory_space=pltpu.SMEM)
VMEM = pl.BlockSpec(memory_space=pltpu.VMEM)
MIB = 1 << 20


def split(x):
    hi = x.astype(jnp.bfloat16)
    lo = (x - hi.astype(jnp.float32)).astype(jnp.bfloat16)
    return hi, lo


def dot3(a, b):
    d = functools.partial(jnp.dot, preferred_element_type=jnp.float32)
    return d(a[0], b[0]) + (d(a[0], b[1]) + d(a[1], b[0]))


def inner_kernel(blocks_ref, prolong_ref, out_ref):
    left = split(prolong_ref[0].T)
    for k in range(blocks_ref.shape[1]):
        out_ref[0, k] = dot3(left, split(blocks_ref[0, k]))


def inner_products(blocks, prolong):
    rows, slots, tile, _ = blocks.shape
    return pl.pallas_call(
        inner_kernel,
        grid=(rows,),
        in_specs=[
            pl.BlockSpec((1, slots, tile, tile), lambda i: (i, 0, 0, 0)),
            pl.BlockSpec((1, tile, tile), lambda i: (i, 0, 0)),
        ],
        out_specs=pl.BlockSpec((1, slots, tile, tile), lambda i: (i, 0, 0, 0)),
        out_shape=jax.ShapeDtypeStruct(blocks.shape, jnp.float32),
        cost_estimate=pl.CostEstimate(
            flops=6 * rows * slots * tile**3, bytes_accessed=9 * MIB, transcendentals=0
        ),
        name="inner",
    )(blocks, prolong)


def pick_kernel(steps, halves, pick_ref, a_ref, b_ref, out_ref, sems):
    peers = out_ref.shape[0]

    def copy(src, tile, y, s, p):
        at = (y * out_ref.shape[1] + s) * CAP + p
        return pltpu.make_async_copy(src.at[tile], out_ref.at[y, s, p], sems.at[at])

    places = [(y, s, p) for y in range(peers) for s in range(len(steps)) for p in range(CAP)]
    for y, s, p in places:
        tile = pick_ref[y, 2 * steps[s] + p]
        if halves:
            half = a_ref.shape[0]

            @pl.when(tile < half)
            def _():
                copy(a_ref, tile, y, s, p).start()

            @pl.when(tile >= half)
            def _():
                copy(b_ref, tile - half, y, s, p).start()
        else:
            copy((a_ref, b_ref)[s], tile, y, s, p).start()
    for y, s, p in places:
        copy(a_ref, 0, y, s, p).wait()


def pick(picks, a, b, steps, halves=False):
    peers = picks.shape[0]
    shape = (peers, len(steps), CAP, *a.shape[1:])
    return pl.pallas_call(
        functools.partial(pick_kernel, steps, halves),
        in_specs=[SMEM, ANY, ANY],
        out_specs=ANY,
        out_shape=jax.ShapeDtypeStruct(shape, jnp.float32),
        scratch_shapes=[pltpu.SemaphoreType.DMA((peers * len(steps) * CAP,))],
        name="pick",
    )(picks, a, b)


def terms_kernel(slot_ref, inner_ref, *refs):
    parts, (out_ref, most_ref, tiles, sems) = refs[:-4], refs[-4:]
    at = 0
    copies = []
    for n, part in enumerate(parts):
        count = part.shape[0]
        copies.append(pltpu.make_async_copy(part, tiles.at[pl.ds(at, count)], sems.at[n]))
        at += count
    for c in copies:
        c.start()
    wide = out_ref.shape[0]
    tile = out_ref.shape[-1]

    def clear(e, _):
        out_ref[e] = jnp.zeros((tile, tile), jnp.float32)
        return 0

    lax.fori_loop(0, wide, clear, 0)
    for c in copies:
        c.wait()

    def one(s, _):
        @pl.when(slot_ref[0, s] >= 0)
        def _():
            term = dot3(split(inner_ref[s]), split(tiles[slot_ref[0, s]]))
            e = slot_ref[1, s]
            out_ref[e] = out_ref[e] + term

        return 0

    lax.fori_loop(0, inner_ref.shape[0], one, 0)
    half = wide // AGD
    most = jnp.float32(0)
    for c in range(AGD):
        total = lax.fori_loop(
            0, half, lambda e, t: t + jnp.abs(out_ref[c * half + e]), jnp.zeros((tile, tile), jnp.float32)
        )
        most = jnp.maximum(most, jnp.max(jnp.sum(total, axis=1)))
    most_ref[...] = jnp.full(most_ref.shape, most, jnp.float32)


def sum_terms(slots, inner, parts, wide):
    tile = inner.shape[-1]
    return pl.pallas_call(
        terms_kernel,
        in_specs=[SMEM, VMEM] + [ANY] * len(parts),
        out_specs=[VMEM, VMEM],
        out_shape=[
            jax.ShapeDtypeStruct((wide, tile, tile), jnp.float32),
            jax.ShapeDtypeStruct((1, tile), jnp.float32),
        ],
        scratch_shapes=[
            pltpu.VMEM((sum(p.shape[0] for p in parts), tile, tile), jnp.float32),
            pltpu.SemaphoreType.DMA((len(parts),)),
        ],
        compiler_params=pltpu.CompilerParams(vmem_limit_bytes=40 * MIB),
        name="terms",
    )(slots, inner, *parts)


def wanted_ends(cols, live, owners, rows):
    hit = live[:, :, None] & (cols[:, :, None] // rows == owners[None, None, :])
    local = (cols % rows)[:, :, None]
    low = jnp.min(jnp.where(hit, local, rows - 1), axis=1)
    high = jnp.max(jnp.where(hit, local, 0), axis=1)
    return low, high


def per_device(blocks, prolong, counts, columns, aggregates):
    rows, slots = columns.shape
    tile = blocks.shape[-1]
    ny, nz = lax.axis_size("col_0"), lax.axis_size("col_1")
    my_y, my_z = lax.axis_index("col_0"), lax.axis_index("col_1")
    peers = ny * nz
    flat = rows * slots
    live = jnp.arange(slots, dtype=jnp.int32)[None, :] < counts[:, None]
    live = live.reshape(1, flat)
    cols = columns.reshape(1, flat)
    note = jnp.concatenate([jnp.where(live, cols, -1), aggregates[None, :]], axis=1)
    note = jnp.pad(note, ((0, 0), (0, 128 - flat - rows)))
    notes = lax.all_to_all(
        jnp.broadcast_to(note, (peers, 128)), COL, split_axis=0, concat_axis=0, tiled=True
    )
    inner = inner_products(blocks, prolong)
    around = [[(i, (i + d) % nz) for i in range(nz)] for d in (1, -1)]
    hop = lambda x, way: lax.ppermute(x, "col_1", around[way])
    theirs = lax.dynamic_slice_in_dim(notes.reshape(ny, nz, 128), my_z, 1, 1)[:, 0, :flat]
    apart = jnp.arange(nz, dtype=jnp.int32)
    owners = my_y * nz + (my_z + apart) % nz
    low, high = wanted_ends(theirs, theirs >= 0, owners, rows)
    picks = jnp.stack([low, high], axis=-1).reshape(ny, nz * CAP)
    swap = lambda x: lax.all_to_all(x, "col_0", split_axis=0, concat_axis=0, tiled=True)
    parts = [swap(pick(picks, prolong, prolong, (0,)))]
    up = down = prolong
    for r in range(1, nz // 2):
        up, down = hop(up, 0), hop(down, 1)
        parts.append(swap(pick(picks, up, down, (nz - r, r))))
    up, down = hop(up[: rows // 2], 0), hop(down[rows // 2 :], 1)
    parts.append(swap(pick(picks, up, down, (nz // 2,), halves=True)))
    parts = [p.reshape(-1, tile, tile) for p in parts]
    owner, within = cols // rows, cols % rows
    same = (owner.T == owner) & live
    first = jnp.min(jnp.where(same, within, rows), axis=1)[None, :]
    second = (within > first).astype(jnp.int32)
    ahead = (owner % nz - my_z) % nz
    r = jnp.minimum(ahead, nz - ahead)
    alone = (r == 0) | (r == nz // 2)
    base = jnp.where(r == 0, 0, (2 * r - 1) * ny * CAP)
    at_set = jnp.where(alone, owner // nz, owner // nz * 2 + (ahead == r).astype(jnp.int32))
    source = jnp.where(live, base + at_set * CAP + second, -1)
    slab_agg = notes[:, flat : flat + rows]
    hot = (owner.T[:, :, None] == jnp.arange(peers)[None, :, None]) & (
        within.T[:, :, None] == jnp.arange(rows)[None, None, :]
    )
    col_agg = jnp.sum(jnp.where(hot, slab_agg[None], 0), axis=(1, 2))[None, :]
    row_agg = jnp.broadcast_to(aggregates[:, None], (rows, slots)).reshape(1, flat)
    target = row_agg * (AGD * peers) + owner * AGD + col_agg
    where = jnp.concatenate([source, target], axis=0).astype(jnp.int32)
    galerkin, most = sum_terms(where, inner.reshape(flat, tile, tile), parts, AGD * AGD * peers)
    everyone = lax.axis_size(ROW_COL)
    all_most = lax.all_to_all(
        jnp.broadcast_to(most, (everyone, tile)), ROW_COL, split_axis=0, concat_axis=0, tiled=True
    )
    bound = jnp.max(all_most)
    return galerkin.reshape(AGD, AGD * peers, tile, tile) / (bound + 1e-06)


def solution(mesh):
    torus = Mesh(mesh.devices.reshape(4, 2, 4, 8), ("row_0", "row_1", "col_0", "col_1"))
    placed = (
        P(ROW_COL, None, None, None),
        P(ROW_COL, None, None),
        P(ROW_COL),
        P(ROW_COL, None),
        P(ROW_COL),
    )
    return jax.shard_map(
        per_device,
        mesh=torus,
        in_specs=placed,
        out_specs=P(ROW_COL, None, None, None),
        check_vma=False,
    )
```

time: 220 us -> 277 us (1.26)
  the two profiles are of different devices: /device:TPU:8 before, /device:TPU:1 now
where the time goes in v1:
time: 277 us
  Pallas kernels  159 us (57%)
  starting transfers between devices  39.4 us (14%)
  blocking collectives  30.1 us (11%)
  waiting for transfers between devices  25.4 us (9%)
  other arithmetic  11.2 us (4%)
  local copies, waits for them, and re-layouts  10.9 us (4%)
    pallas_call x5, Pallas kernels, pick(): pl.pallas_call(functools.partial(pick_kernel, steps, halves), in_specs=[S...  137 us
    all_to_all x1, blocking collectives, per_device(): lax.all_to_all(jnp.broadcast_to(most, (everyone, tile)), ROW_COL, split_a...  30.1 us
    all_to_all x5, starting transfers between devices, per_device(): lax.all_to_all(x, 'col_0', split_axis=0, concat_axis=0, tiled=True)  20.1 us
    ppermute x8, waiting for transfers between devices, per_device(): hop = lambda x, way: lax.ppermute(x, 'col_1', around[way])  15.6 us
    pallas_call x1, Pallas kernels, sum_terms(): pl.pallas_call(terms_kernel, in_specs=[SMEM, VMEM] + [ANY] * len(parts),...  14 us
    ppermute x8, starting transfers between devices, per_device(): hop = lambda x, way: lax.ppermute(x, 'col_1', around[way])  12.2 us
    all_to_all x1, waiting for transfers between devices, per_device(): lax.all_to_all(jnp.broadcast_to(note, (peers, 128)), COL, split_axis=0, c...  8.54 us
    div x1, other arithmetic, per_device(): return galerkin.reshape(AGD, AGD * peers, tile, tile) / (bound + 1e-06)  8.41 us
  transfers between devices with their start and end apart: 14, of which 5 were waited for; matrix products, arithmetic and copies ran while one was open for 2% of the time, Pallas kernels for 52%

profile of v1, /device:TPU:1, one launch (start us, length us, event | category | flops | bytes accessed | tf_op | source)
XLA Modules:
  0.0 276.6 jit_solution(4758494669604213283)
XLA Ops:
  0.0 6.4 %collective-permute-start.1 = (f32[8,128,128]{2,1,0:T(8,128)}, f32[8,128,128]{2,1,0:T(8,128)S(1)}, u32[]{:S(2)}, u32[]{:S(2)}) collective-permute-start(f32[8,128,128]{2,1,0:T(8,128)} %b_ref.1), channel_id=1, source_target_pairs={{0,7},{1,0},{2,1},{3,2},{4,3},{5,4},{6,5},{7,6},{8,15},{9,8},{10,9... | collective-permute-start | bytes 1572872 | tf_op jit(solution)/shard_map/ppermute | solution.py:180
  6.4 0.0 collective-permute-start
  6.4 0.8 reshape.762
  7.2 0.8 reshape.761
  7.9 0.7 iota_compare_fusion.2
  8.7 0.1 lt.73
  8.8 0.1 lt.69
  8.9 0.2 select_reduce_fusion.1
  9.1 0.7 pad_add_fusion.2
  9.8 0.6 broadcast_in_dim.80
  10.5 7.1 %all-to-all-start = ((s32[32,1,128]{2,1,0:T(1,128)}), s32[32,1,128]{2,1,0:T(1,128)S(1)}, u32[]{:S(2)}, u32[]{:S(2)}) async-start(s32[32,1,128]{2,1,0:T(1,128)} %broadcast_in_dim.80), calls=%async_computation | async-start | bytes 32768 | tf_op jit(solution)/shard_map/all_to_all | solution.py:175
  17.6 8.5 %all-to-all-done = s32[32,1,128]{2,1,0:T(1,128)S(1)} async-done(((s32[32,1,128]{2,1,0:T(1,128)}), s32[32,1,128]{2,1,0:T(1,128)S(1)}, u32[]{:S(2)}, u32[]{:S(2)}) %all-to-all-start) | async-done | bytes 16416 | tf_op jit(solution)/shard_map/all_to_all | solution.py:175
  26.1 0.3 select_reduce_fusion.3
  26.4 0.1 copy.24
  26.5 0.7 copy.25.pick_ref
  27.2 17.7 %pick.5 = f32[4,1,2,128,128]{4,3,2,1,0:T(8,128)} custom-call(s32[4,16]{1,0:T(4,128)} %copy.25.pick_ref, f32[8,128,128]{2,1,0:T(8,128)} %b_ref.1, f32[8,128,128]{2,1,0:T(8,128)} %b_ref.1), custom_call_target="tpu_custom_call" | custom-call | tf_op jit(solution)/shard_map/pick/pallas_call | solution.py:85
  44.9 0.0 copy-start.10
  45.0 3.5 %all-to-all-start.1 = ((f32[4,1,2,128,128]{4,3,2,1,0:T(8,128)}), f32[4,1,2,128,128]{4,3,2,1,0:T(8,128)S(1)}, u32[]{:S(2)}, u32[]{:S(2)}) async-start(f32[4,1,2,128,128]{4,3,2,1,0:T(8,128)} %pick.5), calls=%async_computation.1 | async-start | bytes 1048576 | tf_op jit(solution)/shard_map/all_to_all | solution.py:186
  48.4 0.0 collective-permute-done.1.b_ref
  48.5 0.0 copy-start.8
  48.5 0.0 collective-permute-done.a_ref
  48.5 0.8 copy-done.8
  49.2 0.8 copy-done.7
  50.0 33.7 %pick.6 = f32[4,2,2,128,128]{4,3,2,1,0:T(8,128)} custom-call(s32[4,16]{1,0:T(4,128)} %copy.25.pick_ref, f32[8,128,128]{2,1,0:T(8,128)} %copy-done.7, f32[8,128,128]{2,1,0:T(8,128)} %copy-done.8), custom_call_target="tpu_custom_call" | custom-call | tf_op jit(solution)/shard_map/pick/pallas_call | solution.py:85
  83.8 0.0 all-to-all-done.1
  83.8 0.8 copy-done.1
  84.6 4.2 %all-to-all-start.2 = ((f32[4,2,2,128,128]{4,3,2,1,0:T(8,128)}), f32[4,2,2,128,128]{4,3,2,1,0:T(8,128)S(1)}, u32[]{:S(2)}, u32[]{:S(2)}) async-start(f32[4,2,2,128,128]{4,3,2,1,0:T(8,128)} %pick.6), calls=%async_computation.2 | async-start | bytes 2097152 | tf_op jit(solution)/shard_map/all_to_all | solution.py:186
  88.8 0.3 collective-permute-start.3
  89.0 1.2 collective-permute-start.2
  90.2 9.0 %collective-permute-done.3.b_ref = f32[8,128,128]{2,1,0:T(8,128)} collective-permute-done((f32[8,128,128]{2,1,0:T(8,128)}, f32[8,128,128]{2,1,0:T(8,128)}, u32[]{:S(2)}, u32[]{:S(2)}) %collective-permute-start.3) | collective-permute-done | bytes 524320 | tf_op jit(solution)/shard_map/ppermute | solution.py:180
  99.3 1.5 collective-permute-start.5
  100.7 0.0 collective-permute-done.2.a_ref
  100.7 0.0 collective-permute-start.4
  100.7 33.7 %pick.7 = f32[4,2,2,128,128]{4,3,2,1,0:T(8,128)} custom-call(s32[4,16]{1,0:T(4,128)} %copy.25.pick_ref, f32[8,128,128]{2,1,0:T(8,128)} %collective-permute-done.2.a_ref, f32[8,128,128]{2,1,0:T(8,128)} %collective-permute-done.3.b_ref), custom_call_target="tpu_custom_call" | custom-call | tf_op jit(solution)/shard_map/pick/pallas_call | solution.py:85
  134.5 0.0 all-to-all-done.2
  134.5 4.0 %all-to-all-start.3 = ((f32[4,2,2,128,128]{4,3,2,1,0:T(8,128)}), f32[4,2,2,128,128]{4,3,2,1,0:T(8,128)S(1)}, u32[]{:S(2)}, u32[]{:S(2)}) async-start(f32[4,2,2,128,128]{4,3,2,1,0:T(8,128)} %pick.7), calls=%async_computation.3 | async-start | bytes 2097152 | tf_op jit(solution)/shard_map/all_to_all | solution.py:186
  138.4 0.0 collective-permute-done.5.b_ref
  138.5 2.7 collective-permute-start.7
  141.2 0.0 collective-permute-done.4.a_ref
  141.2 0.1 collective-permute-start.6
  141.3 3.2 %collective-permute-done.7.b_ref = f32[4,128,128]{2,1,0:T(8,128)S(1)} collective-permute-done((f32[4,128,128]{2,1,0:T(8,128)S(1)}, f32[4,128,128]{2,1,0:T(8,128)S(1)}, u32[]{:S(2)}, u32[]{:S(2)}) %collective-permute-start.7) | collective-permute-done | bytes 262176 | tf_op jit(solution)/shard_map/ppermute | solution.py:180
  144.5 3.3 %collective-permute-done.6.a_ref = f32[4,128,128]{2,1,0:T(8,128)} collective-permute-done((f32[4,128,128]{2,1,0:T(8,128)S(1)}, f32[4,128,128]{2,1,0:T(8,128)}, u32[]{:S(2)}, u32[]{:S(2)}) %collective-permute-start.6) | collective-permute-done | bytes 262176 | tf_op jit(solution)/shard_map/ppermute | solution.py:180
  147.9 17.7 %pick.9 = f32[4,1,2,128,128]{4,3,2,1,0:T(8,128)} custom-call(s32[4,16]{1,0:T(4,128)} %copy.25.pick_ref, f32[4,128,128]{2,1,0:T(8,128)} %collective-permute-done.6.a_ref, f32[4,128,128]{2,1,0:T(8,128)} %copy-done.9), custom_call_target="tpu_custom_call" | custom-call | tf_op jit(solution)/shard_map/pick/pallas_call | solution.py:85
  165.6 0.0 all-to-all-done.3
  165.6 4.2 %all-to-all-start.5 = ((f32[4,1,2,128,128]{4,3,2,1,0:T(8,128)}), f32[4,1,2,128,128]{4,3,2,1,0:T(8,128)S(1)}, u32[]{:S(2)}, u32[]{:S(2)}) async-start(f32[4,1,2,128,128]{4,3,2,1,0:T(8,128)} %pick.9), calls=%async_computation.5 | async-start | bytes 1048576 | tf_op jit(solution)/shard_map/all_to_all | solution.py:186
  169.9 33.7 %pick.8 = f32[4,2,2,128,128]{4,3,2,1,0:T(8,128)} custom-call(s32[4,16]{1,0:T(4,128)} %copy.25.pick_ref, f32[8,128,128]{2,1,0:T(8,128)} %copy-done.6, f32[8,128,128]{2,1,0:T(8,128)} %copy-done.5), custom_call_target="tpu_custom_call" | custom-call | tf_op jit(solution)/shard_map/pick/pallas_call | solution.py:85
  203.6 0.0 all-to-all-done.5
  203.6 0.0 copy-start.3
  203.6 0.8 copy-done.3
  204.4 4.2 %all-to-all-start.4 = ((f32[4,2,2,128,128]{4,3,2,1,0:T(8,128)}), f32[4,2,2,128,128]{4,3,2,1,0:T(8,128)S(1)}, u32[]{:S(2)}, u32[]{:S(2)}) async-start(f32[4,2,2,128,128]{4,3,2,1,0:T(8,128)} %pick.8), calls=%async_computation.4 | async-start | bytes 2097152 | tf_op jit(solution)/shard_map/all_to_all | solution.py:186
  208.7 0.1 broadcast_in_dim.78
  208.7 0.1 mul.83
  208.8 8.1 %inner.1 = f32[8,8,128,128]{3,2,1,0:T(8,128)} custom-call(f32[8,8,128,128]{3,2,1,0:T(8,128)} %blocks_ref.1, f32[8,128,128]{2,1,0:T(8,128)} %b_ref.1), custom_call_target="tpu_custom_call" | custom-call | flops 805306368 | bytes 9437184 | tf_op jit(solution)/shard_map/inner/pallas_call | solution.py:40
  216.9 0.1 slice.16
  217.0 0.1 select_reduce_fusion
  217.1 1.3 all-to-all-done.4
  218.4 2.2 copy-done
  220.6 1.0 copy-done.2
  221.6 1.0 copy-done.4
  222.7 14.0 %terms.1 = (f32[128,128,128]{2,1,0:T(8,128)}, f32[1,128]{1,0:T(1,128)S(1)}) custom-call(s32[2,64]{1,0:T(2,128)S(1)} %pad_add_fusion.1.slot_ref, f32[64,128,128]{2,1,0:T(8,128)S(1)} %bitcast.24, f32[8,128,128]{2,1,0:T(8,128)S(1)} %bitcast.28, f32[16,128,128]{2,1,0:T(8,128)S(1)} %bitcast.25, f32[16,128,128]{2,1,0:T(8,128)S(1)} %bitcast.26, ...), custom_call_target="tpu_custom_call" | custom-call | tf_op jit(solution)/shard_map/terms/pallas_call | solution.py:138
  236.7 0.1 broadcast_in_dim.86
  236.8 30.1 %all_to_all.40 = f32[256,1,128]{2,1,0:T(1,128)S(1)} all-to-all(f32[256,1,128]{2,1,0:T(1,128)S(1)} %broadcast_in_dim.86), channel_id=1, replica_groups=mesh['row_0'=4,'row_1'=2,'col_0'=4,'col_1'=8] {'row_0','row_1','col_0','..., dimensions={0} | all-to-all | bytes 262144 | tf_op jit(solution)/shard_map/all_to_all | solution.py:215
  266.9 0.6 reduce_max.19
  268.1 8.4 %broadcast_divide_fusion = f32[128,128,128]{2,1,0:T(8,128)} fusion(f32[128,128,128]{2,1,0:T(8,128)} %get-tuple-element.7, f32[]{:T(128)S(6)} %add.214), kind=kLoop, calls=%fused_computation | loop fusion | flops 2097152 | bytes 16777220 | tf_op jit(solution)/shard_map/div | solution.py:219
  (27 shorter events, 0.2 us)
Async XLA Ops:
  0.0 48.4 %collective-permute-start.1 = (f32[8,128,128]{2,1,0:T(8,128)}, f32[8,128,128]{2,1,0:T(8,128)S(1)}, u32[]{:S(2)}, u32[]{:S(2)}) collective-permute-start(f32[8,128,128]{2,1,0:T(8,128)} %b_ref.1), channel_id=1, source_target_pairs={{0,7},{1,0},{2,1},{3,2},{4,3},{5,4},{6,5},{7,6},{8,15},{9,8},{10,9... | collective-permute-start | bytes 1572872 | tf_op jit(solution)/shard_map/ppermute | solution.py:180
  6.4 42.1 %collective-permute-start = (f32[8,128,128]{2,1,0:T(8,128)}, f32[8,128,128]{2,1,0:T(8,128)S(1)}, u32[]{:S(2)}, u32[]{:S(2)}) collective-permute-start(f32[8,128,128]{2,1,0:T(8,128)} %b_ref.1), channel_id=1, source_target_pairs={{0,1},{1,2},{2,3},{3,4},{4,5},{5,6},{6,7},{7,0},{8,9},{9,10},{10,1... | collective-permute-start | bytes 1572872 | tf_op jit(solution)/shard_map/ppermute | solution.py:180
  10.5 15.7 %all-to-all-start = ((s32[32,1,128]{2,1,0:T(1,128)}), s32[32,1,128]{2,1,0:T(1,128)S(1)}, u32[]{:S(2)}, u32[]{:S(2)}) async-start(s32[32,1,128]{2,1,0:T(1,128)} %broadcast_in_dim.80), calls=%async_computation | async-start | bytes 32768 | tf_op jit(solution)/shard_map/all_to_all | solution.py:175
  44.9 163.7 %copy-start.10 = (s32[8]{0:T(128)S(1)}, s32[8]{0:T(128)}, u32[]{:S(2)}) copy-start(s32[8]{0:T(128)} %param.9) | copy-start | bytes 100
  45.0 38.8 %all-to-all-start.1 = ((f32[4,1,2,128,128]{4,3,2,1,0:T(8,128)}), f32[4,1,2,128,128]{4,3,2,1,0:T(8,128)S(1)}, u32[]{:S(2)}, u32[]{:S(2)}) async-start(f32[4,1,2,128,128]{4,3,2,1,0:T(8,128)} %pick.5), calls=%async_computation.1 | async-start | bytes 1048576 | tf_op jit(solution)/shard_map/all_to_all | solution.py:186
  48.5 0.8 copy-start.8
  49.2 0.8 copy-start.7
  83.8 0.8 copy-start.1
  84.6 49.9 %all-to-all-start.2 = ((f32[4,2,2,128,128]{4,3,2,1,0:T(8,128)}), f32[4,2,2,128,128]{4,3,2,1,0:T(8,128)S(1)}, u32[]{:S(2)}, u32[]{:S(2)}) async-start(f32[4,2,2,128,128]{4,3,2,1,0:T(8,128)} %pick.6), calls=%async_computation.2 | async-start | bytes 2097152 | tf_op jit(solution)/shard_map/all_to_all | solution.py:186
  88.8 10.5 %collective-permute-start.3 = (f32[8,128,128]{2,1,0:T(8,128)}, f32[8,128,128]{2,1,0:T(8,128)}, u32[]{:S(2)}, u32[]{:S(2)}) collective-permute-start(f32[8,128,128]{2,1,0:T(8,128)} %copy-done.8), channel_id=1, source_target_pairs={{0,7},{1,0},{2,1},{3,2},{4,3},{5,4},{6,5},{7,6},{8,15},{9,8},{10,9... | collective-permute-start | bytes 1572872 | tf_op jit(solution)/shard_map/ppermute | solution.py:180
  89.0 11.7 %collective-permute-start.2 = (f32[8,128,128]{2,1,0:T(8,128)}, f32[8,128,128]{2,1,0:T(8,128)}, u32[]{:S(2)}, u32[]{:S(2)}) collective-permute-start(f32[8,128,128]{2,1,0:T(8,128)} %copy-done.7), channel_id=1, source_target_pairs={{0,1},{1,2},{2,3},{3,4},{4,5},{5,6},{6,7},{7,0},{8,9},{9,10},{10,1... | collective-permute-start | bytes 1572872 | tf_op jit(solution)/shard_map/ppermute | solution.py:180
  99.3 39.2 %collective-permute-start.5 = (f32[8,128,128]{2,1,0:T(8,128)}, f32[8,128,128]{2,1,0:T(8,128)S(1)}, u32[]{:S(2)}, u32[]{:S(2)}) collective-permute-start(f32[8,128,128]{2,1,0:T(8,128)} %collective-permute-done.3.b_ref), channel_id=1, source_target_pairs={{0,7},{1,0},{2,1},{3,2},{4,3},{5,4},{6,5},{7,6},{8,15},{9,8},{10,9... | collective-permute-start | bytes 1572872 | tf_op jit(solution)/shard_map/ppermute | solution.py:180
  100.7 40.5 %collective-permute-start.4 = (f32[8,128,128]{2,1,0:T(8,128)}, f32[8,128,128]{2,1,0:T(8,128)S(1)}, u32[]{:S(2)}, u32[]{:S(2)}) collective-permute-start(f32[8,128,128]{2,1,0:T(8,128)} %collective-permute-done.2.a_ref), channel_id=1, source_target_pairs={{0,1},{1,2},{2,3},{3,4},{4,5},{5,6},{6,7},{7,0},{8,9},{9,10},{10,1... | collective-permute-start | bytes 1572872 | tf_op jit(solution)/shard_map/ppermute | solution.py:180
  134.5 31.2 %all-to-all-start.3 = ((f32[4,2,2,128,128]{4,3,2,1,0:T(8,128)}), f32[4,2,2,128,128]{4,3,2,1,0:T(8,128)S(1)}, u32[]{:S(2)}, u32[]{:S(2)}) async-start(f32[4,2,2,128,128]{4,3,2,1,0:T(8,128)} %pick.7), calls=%async_computation.3 | async-start | bytes 2097152 | tf_op jit(solution)/shard_map/all_to_all | solution.py:186
  138.4 31.5 %copy-start.5 = (f32[8,128,128]{2,1,0:T(8,128)}, f32[8,128,128]{2,1,0:T(8,128)S(1)}, u32[]{:S(2)}) copy-start(f32[8,128,128]{2,1,0:T(8,128)S(1)} %collective-permute-done.5.b_ref) | copy-start | bytes 1572868
  138.5 6.1 %collective-permute-start.7 = (f32[4,128,128]{2,1,0:T(8,128)S(1)}, f32[4,128,128]{2,1,0:T(8,128)S(1)}, u32[]{:S(2)}, u32[]{:S(2)}) collective-permute-start(f32[4,128,128]{2,1,0:T(8,128)S(1)} %slice.18), channel_id=1, source_target_pairs={{0,7},{1,0},{2,1},{3,2},{4,3},{5,4},{6,5},{7,6},{8,15},{9,8},{10,9... | collective-permute-start | bytes 786440 | tf_op jit(solution)/shard_map/ppermute | solution.py:180
  141.2 24.4 %copy-start.6 = (f32[8,128,128]{2,1,0:T(8,128)}, f32[8,128,128]{2,1,0:T(8,128)S(1)}, u32[]{:S(2)}) copy-start(f32[8,128,128]{2,1,0:T(8,128)S(1)} %collective-permute-done.4.a_ref) | copy-start | bytes 1572868
  141.2 6.6 %collective-permute-start.6 = (f32[4,128,128]{2,1,0:T(8,128)S(1)}, f32[4,128,128]{2,1,0:T(8,128)}, u32[]{:S(2)}, u32[]{:S(2)}) collective-permute-start(f32[4,128,128]{2,1,0:T(8,128)S(1)} %slice.17), channel_id=1, source_target_pairs={{0,1},{1,2},{2,3},{3,4},{4,5},{5,6},{6,7},{7,0},{8,9},{9,10},{10,1... | collective-permute-start | bytes 786440 | tf_op jit(solution)/shard_map/ppermute | solution.py:180
  144.5 3.3 %copy-start.9 = (f32[4,128,128]{2,1,0:T(8,128)}, f32[4,128,128]{2,1,0:T(8,128)S(1)}, u32[]{:S(2)}) copy-start(f32[4,128,128]{2,1,0:T(8,128)S(1)} %collective-permute-done.7.b_ref) | copy-start | bytes 786436
  165.6 38.0 %all-to-all-start.5 = ((f32[4,1,2,128,128]{4,3,2,1,0:T(8,128)}), f32[4,1,2,128,128]{4,3,2,1,0:T(8,128)S(1)}, u32[]{:S(2)}, u32[]{:S(2)}) async-start(f32[4,1,2,128,128]{4,3,2,1,0:T(8,128)} %pick.9), calls=%async_computation.5 | async-start | bytes 1048576 | tf_op jit(solution)/shard_map/all_to_all | solution.py:186
  203.6 0.8 copy-start.3
  204.4 14.0 %all-to-all-start.4 = ((f32[4,2,2,128,128]{4,3,2,1,0:T(8,128)}), f32[4,2,2,128,128]{4,3,2,1,0:T(8,128)S(1)}, u32[]{:S(2)}, u32[]{:S(2)}) async-start(f32[4,2,2,128,128]{4,3,2,1,0:T(8,128)} %pick.8), calls=%async_computation.4 | async-start | bytes 2097152 | tf_op jit(solution)/shard_map/all_to_all | solution.py:186
  218.4 2.2 copy-start
  220.6 1.0 copy-start.2
  221.6 1.0 copy-start.4

commit v2 on v1

v2 whole, which is shorter than its diff:
```python
import functools

import jax
import jax.numpy as jnp
from jax import lax
from jax.experimental import pallas as pl
from jax.experimental.pallas import tpu as pltpu
from jax.sharding import Mesh
from jax.sharding import PartitionSpec as P

AGD = 2
CAP = 2
COL = ("col_0", "col_1")
ROW_COL = ("row_0", "row_1", "col_0", "col_1")
ANY = pl.BlockSpec(memory_space=pl.ANY)
SMEM = pl.BlockSpec(memory_space=pltpu.SMEM)
VMEM = pl.BlockSpec(memory_space=pltpu.VMEM)
HBM = pl.BlockSpec(memory_space=pltpu.HBM)
MIB = 1 << 20
UNROLL = 4
CUTS = (1,2)
MERGED = 1
EARLY = 0
LIMIT = 60


def split(x, axis):
    hi = x.astype(jnp.bfloat16)
    lo = (x - hi.astype(jnp.float32)).astype(jnp.bfloat16)
    return jnp.concatenate([hi, lo], axis=axis)


def dot_split(left, right):
    n = right.shape[0]
    four = jnp.dot(left, right, preferred_element_type=jnp.float32)
    return four[:n, :n] + ((four[:n, n:] + four[n:, :n]) + four[n:, n:])


def params(mib):
    return pltpu.CompilerParams(vmem_limit_bytes=mib * MIB)


def inner_kernel(blocks_ref, prolong_ref, out_ref, done_ref):
    left = split(prolong_ref[0].T, 0)
    for k in range(blocks_ref.shape[1]):
        out_ref[0, k] = split(dot_split(left, split(blocks_ref[0, k], 1)), 0)
    done_ref[...] = jnp.zeros_like(done_ref)


def inner_products(blocks, prolong):
    rows, slots, tile, _ = blocks.shape
    return pl.pallas_call(
        inner_kernel,
        grid=(rows,),
        in_specs=[
            pl.BlockSpec((1, slots, tile, tile), lambda i: (i, 0, 0, 0)),
            pl.BlockSpec((1, tile, tile), lambda i: (i, 0, 0)),
        ],
        out_specs=[
            pl.BlockSpec((1, slots, 2 * tile, tile), lambda i: (i, 0, 0, 0)),
            pl.BlockSpec((8, tile), lambda i: (0, 0)),
        ],
        out_shape=[
            pltpu.HBM((rows, slots, 2 * tile, tile), jnp.bfloat16),
            jax.ShapeDtypeStruct((8, tile), jnp.float32),
        ],
        cost_estimate=pl.CostEstimate(
            flops=8 * rows * slots * tile**3, bytes_accessed=9 * MIB, transcendentals=0
        ),
        compiler_params=params(LIMIT),
        name="inner",
    )(blocks, prolong)


def pick_kernel(steps, apart, pick_ref, at_ref, *refs):
    peers = pick_ref.shape[0]
    count = peers if apart else 1
    sources, outs, (sets, sems) = refs[: len(steps)], refs[-2 - count : -2], refs[-2:]
    loads, place = [], {}
    at = 0
    for n, step in enumerate(steps):
        place[step] = place.get(step, at)
        count = sources[n].shape[0]
        loads.append(
            pltpu.make_async_copy(sources[n], sets.at[pl.ds(at, count)], sems.at[n])
        )
        at += count
    for load in loads:
        load.start()
    for n, load in enumerate(loads):
        load.wait()
        if steps[n] in steps[n + 1 :]:
            continue
        s = list(place).index(steps[n])
        for y in range(peers):
            for p in range(CAP):
                if apart:
                    out, peer = outs[y], (at_ref[0] + y) % peers
                else:
                    out, peer = outs[0].at[y], y
                out[CAP * s + p] = sets[place[steps[n]] + pick_ref[peer, CAP * steps[n] + p]]


def pick(picks, at, sets, steps, apart, after):
    peers = picks.shape[0]
    shape = (len(set(steps)) * CAP, *sets[0].shape[1:])
    shapes = [pltpu.HBM(shape, jnp.float32)] * peers
    return pl.pallas_call(
        functools.partial(pick_kernel, steps, apart),
        in_specs=[SMEM, SMEM] + [ANY] * (len(sets) + len(after)),
        out_specs=[VMEM] * peers if apart else [VMEM],
        out_shape=shapes if apart else [pltpu.HBM((peers, *shape), jnp.float32)],
        scratch_shapes=[
            pltpu.VMEM((sum(x.shape[0] for x in sets), *shape[1:]), jnp.float32),
            pltpu.SemaphoreType.DMA((len(sets),)),
        ],
        cost_estimate=pl.CostEstimate(flops=0, bytes_accessed=8 * MIB, transcendentals=0),
        compiler_params=params(LIMIT),
        name="pick",
    )(picks, at, *sets, *after)


def terms_kernel(slot_ref, inner_ref, *refs):
    parts, rest = refs[:-13], refs[-13:]
    out_ref, used_ref, most_ref, left, held, right, sums, most, ids, agg_ref, sem, sems, part_sems = rest
    wide = out_ref.shape[0]
    tile = out_ref.shape[-1]
    load = pltpu.make_async_copy(inner_ref, left, sem)
    copies = []
    at = 0
    for n, part in enumerate(parts):
        count = part.shape[0]
        copies.append(pltpu.make_async_copy(part, held.at[pl.ds(at, count)], part_sems.at[n]))
        copies[-1].start()
        at += count
    load.start()

    def clear(e, _):
        for n in range(8):
            used_ref[8 * e + n] = 0
        return 0

    lax.fori_loop(0, used_ref.shape[0] // 8, clear, 0)
    at = 0
    for part, copy in zip(parts, copies):
        copy.wait()
        for n in range(at, at + part.shape[0]):
            right[n] = split(held[n, :tile], 1)
            ids[n : n + 1] = held[n, tile : tile + 1].astype(jnp.int32)
        at += part.shape[0]
    load.wait()
    look_up = pltpu.make_async_copy(ids, agg_ref, sem)
    look_up.start()
    look_up.wait()
    live = slot_ref[3, 0]

    def some(n, _):
        terms = []
        for m in range(UNROLL):
            s = UNROLL * n + m
            terms.append(dot_split(left[slot_ref[0, s]], right[slot_ref[1, s]]))
        for m in range(UNROLL):
            s = UNROLL * n + m
            e = jnp.where(s < live, slot_ref[2, s] + agg_ref[slot_ref[1, s], 0], wide)

            @pl.when(e < wide)
            def _():
                @pl.when(used_ref[e] == 0)
                def _():
                    count = used_ref[2 * wide]
                    used_ref[e] = 1
                    used_ref[wide + count] = e
                    used_ref[2 * wide] = count + 1
                    sums[e] = jnp.zeros((tile, tile), jnp.float32)

            sums[e] = sums[e] + terms[m]
        return 0

    sums[wide] = jnp.zeros((tile, tile), jnp.float32)
    lax.fori_loop(0, (live + UNROLL - 1) // UNROLL, some, 0)
    most[...] = jnp.zeros_like(most)
    half = wide // AGD
    copy = lambda e: pltpu.make_async_copy(sums.at[e], out_ref.at[e], sems.at[e])

    def look(e):
        copy(e).start()
        most[e // half] = most[e // half] + jnp.abs(sums[e])

    each_used(used_ref, look)
    row_sums = jnp.sum(most[...], axis=2)
    most_ref[...] = jnp.full(most_ref.shape, jnp.max(row_sums), jnp.float32)
    each_used(used_ref, lambda e: copy(e).wait())


def each_used(used_ref, do):
    wide = used_ref.shape[0] // 2 - 4

    def step(n, _):
        do(used_ref[wide + n])
        return 0

    lax.fori_loop(0, used_ref[2 * wide], step, 0)


def sum_terms(slots, inner, parts, wide):
    flat, _, tile = inner.shape
    return pl.pallas_call(
        terms_kernel,
        in_specs=[SMEM, ANY] + [ANY] * len(parts),
        out_specs=[ANY, SMEM, VMEM],
        out_shape=[
            pltpu.HBM((wide, tile, tile), jnp.float32),
            jax.ShapeDtypeStruct((2 * wide + 8,), jnp.int32),
            jax.ShapeDtypeStruct((1, tile), jnp.float32),
        ],
        scratch_shapes=[
            pltpu.VMEM(inner.shape, jnp.bfloat16),
            pltpu.VMEM((flat, *parts[0].shape[1:]), jnp.float32),
            pltpu.VMEM((flat, tile, 2 * tile), jnp.bfloat16),
            pltpu.VMEM((wide + 1, tile, tile), jnp.float32),
            pltpu.VMEM((AGD, tile, tile), jnp.float32),
            pltpu.VMEM((flat, tile), jnp.int32),
            pltpu.SMEM((flat, tile), jnp.int32),
            pltpu.SemaphoreType.DMA,
            pltpu.SemaphoreType.DMA((wide,)),
            pltpu.SemaphoreType.DMA((len(parts),)),
        ],
        cost_estimate=pl.CostEstimate(
            flops=8 * flat * tile**3, bytes_accessed=16 * MIB, transcendentals=0
        ),
        compiler_params=params(LIMIT),
        name="terms",
    )(slots, inner, *parts)


def clear_kernel(used_ref, _, out_ref, zero, sems):
    zero[...] = jnp.zeros_like(zero)
    copy = lambda e: pltpu.make_async_copy(zero, out_ref.at[e], sems.at[e])

    def each(do):
        def step(e, _):
            pl.when(used_ref[e] == 0)(lambda: do(e))
            return 0

        lax.fori_loop(0, out_ref.shape[0], step, 0)

    each(lambda e: copy(e).start())
    each(lambda e: copy(e).wait())


def clear_rest(used, tiles):
    wide, tile, _ = tiles.shape
    return pl.pallas_call(
        clear_kernel,
        in_specs=[SMEM, ANY],
        out_specs=ANY,
        out_shape=pltpu.HBM(tiles.shape, jnp.float32),
        scratch_shapes=[
            pltpu.VMEM((tile, tile), jnp.float32),
            pltpu.SemaphoreType.DMA((wide,)),
        ],
        input_output_aliases={1: 0},
        cost_estimate=pl.CostEstimate(flops=0, bytes_accessed=8 * MIB, transcendentals=0),
        compiler_params=params(LIMIT),
        name="clear",
    )(used, tiles)


def scale_kernel(used_ref, most_ref, _, out_ref, held, come, go):
    get = lambda e: pltpu.make_async_copy(out_ref.at[e], held.at[e], come.at[e])
    put = lambda e: pltpu.make_async_copy(held.at[e], out_ref.at[e], go.at[e])
    factor = 1.0 / (most_ref[0, 0] + 1e-06)

    def one(e):
        get(e).wait()
        held[e] = held[e] * factor
        put(e).start()

    each_used(used_ref, lambda e: get(e).start())
    each_used(used_ref, one)
    each_used(used_ref, lambda e: put(e).wait())


def scale(used, bound, tiles):
    return pl.pallas_call(
        scale_kernel,
        in_specs=[SMEM, SMEM, ANY],
        out_specs=ANY,
        out_shape=pltpu.HBM(tiles.shape, jnp.float32),
        scratch_shapes=[
            pltpu.VMEM(tiles.shape, jnp.float32),
            pltpu.SemaphoreType.DMA((tiles.shape[0],)),
            pltpu.SemaphoreType.DMA((tiles.shape[0],)),
        ],
        input_output_aliases={2: 0},
        compiler_params=params(LIMIT),
        name="scale",
    )(used, bound, tiles)


def wanted_ends(cols, owners, rows):
    cols = cols[..., None]
    hit = (cols >= 0) & (cols // rows == owners)
    low = jnp.min(jnp.where(hit, cols % rows, rows - 1), axis=(1, 2))
    high = jnp.max(jnp.where(hit, cols % rows, 0), axis=(1, 2))
    return low, high


def per_device(blocks, prolong, counts, columns, aggregates):
    rows, slots = columns.shape
    tile = blocks.shape[-1]
    ny, nz = lax.axis_size("col_0"), lax.axis_size("col_1")
    my_y, my_z = lax.axis_index("col_0"), lax.axis_index("col_1")
    peers = ny * nz
    wide = AGD * peers
    flat = rows * slots
    around = [[(i, (i + d) % nz) for i in range(nz)] for d in (1, -1)]
    hop = lambda x, way: lax.ppermute(x, "col_1", around[way])
    swap = lambda x, axis="col_0": lax.all_to_all(x, axis, split_axis=0, concat_axis=0, tiled=True)
    live = jnp.arange(slots, dtype=jnp.int32)[None, :] < counts[:, None]
    tags = jnp.broadcast_to(aggregates.astype(jnp.float32)[:, None, None], (rows, 8, tile))
    tagged = jnp.concatenate([prolong, tags], axis=1)
    up, down = hop(tagged, 0), hop(tagged, 1)
    note = jnp.where(live, columns, -1)
    theirs = swap(jnp.broadcast_to(note, (ny, *note.shape)))
    inner, done = inner_products(blocks, prolong)
    inner = inner.reshape(flat, 2 * tile, tile)
    apart = jnp.arange(nz, dtype=jnp.int32)
    owners = my_y * nz + (my_z + apart) % nz
    low, high = wanted_ends(theirs, owners, rows)
    picks = jnp.stack([low, high], axis=-1).reshape(ny, nz * CAP)
    held = {0: tagged}
    for r in range(1, nz // 2):
        held[nz - r], held[r] = up, down
        far = r == nz // 2 - 1
        up, down = (up[: rows // 2], down[rows // 2 :]) if far else (up, down)
        up, down = hop(up, 0), hop(down, 1)
    orders, parts = [[0]], []
    for r in range(1, nz // 2):
        orders[-1] += [nz - r, r]
        if r in CUTS:
            orders.append([])
    orders[-1].append(nz // 2)
    at = my_y[None]
    onward = lambda x, d: lax.ppermute(x, "col_0", [(i, (i + d) % ny) for i in range(ny)])
    for n, steps in enumerate(orders):
        last = nz // 2 in steps
        sets = [held[d] for d in steps if d in held] + ([up, down] if last else [])
        sent = pick(picks, at, sets, tuple(steps + steps[-1:] * last), n >= MERGED, (done,) * (n == EARLY))
        if n >= MERGED:
            parts += [sent[0]] + [onward(sent[d], d) for d in range(1, ny)]
        else:
            parts.append(swap(sent[0]).reshape(-1, *tagged.shape[1:]))
    cols = columns.reshape(1, flat)
    live = live.reshape(1, flat)
    owner, within = cols // rows, cols % rows
    same = (owner.T == owner) & live
    first = jnp.min(jnp.where(same, within, rows), axis=1)[None, :]
    second = (within > first).astype(jnp.int32)
    ahead = (owner % nz - my_z) % nz
    source, base = jnp.zeros_like(owner), 0
    for n, steps in enumerate(orders):
        peer = (my_y - owner // nz) % ny if n >= MERGED else owner // nz
        for s, step in enumerate(steps):
            there = base + (peer * len(steps) + s) * CAP + second
            source = jnp.where(ahead == step, there, source)
        base += len(steps) * ny * CAP
    row_agg = jnp.broadcast_to(aggregates[:, None], (rows, slots)).reshape(1, flat)
    target = row_agg * wide + owner * AGD
    number = jnp.arange(flat, dtype=jnp.int32)[None, :]
    place = jnp.sum(jnp.where((number < number.T) & live, 1, 0), axis=1)[:, None]
    moved = (place == number) & live.T
    front = lambda x, rest: jnp.sum(jnp.where(moved, x.T - rest, 0), axis=0)[None, :] + rest
    total = jnp.broadcast_to(jnp.sum(live.astype(jnp.int32)), (1, flat))
    where = jnp.concatenate(
        [front(number, 0), front(source, 0), front(target, AGD * wide), total], axis=0
    ).astype(jnp.int32)
    tiles, used, most = sum_terms(where, inner, parts, AGD * wide)
    everyone = lax.axis_size(ROW_COL)
    all_most = swap(jnp.broadcast_to(most, (everyone, tile)), ROW_COL)
    bound = jnp.max(all_most).reshape(1, 1)
    return scale(used, bound, clear_rest(used, tiles)).reshape(AGD, wide, tile, tile)


def solution(mesh):
    torus = Mesh(mesh.devices.reshape(4, 2, 4, 8), ("row_0", "row_1", "col_0", "col_1"))
    placed = (
        P(ROW_COL, None, None, None),
        P(ROW_COL, None, None),
        P(ROW_COL),
        P(ROW_COL, None),
        P(ROW_COL),
    )
    return jax.shard_map(
        per_device,
        mesh=torus,
        in_specs=placed,
        out_specs=P(ROW_COL, None, None, None),
        check_vma=False,
    )
```

time: 277 us -> 132 us (0.48)
  Pallas kernels: 159 us -> 40 us
  blocking collectives: 30.1 us -> 0 us
  waiting for transfers between devices: 25.4 us -> 35 us
  other arithmetic: 11.2 us -> 5.18 us
  local copies, waits for them, and re-layouts: 10.9 us -> 4.89 us
  starting transfers between devices: 39.4 us -> 45.2 us
    pallas_call x6, Pallas kernels: 151 us -> 31.8 us  [the longest x1 11.9 us: sum_terms(): pl.pallas_call(terms_kernel, in_specs=[SMEM, ANY] + [ANY] * len(parts), o...]
    all_to_all x1 -> x0, blocking collectives: 30.1 us -> none  [per_device(): lax.all_to_all(jnp.broadcast_to(most, (everyone, tile)), ROW_COL, split_a...]
    ppermute x0 -> x6, waiting for transfers between devices: none -> 16.6 us  [per_device(): lax.ppermute(x, 'col_0', [(i, (i + d) % ny) for i in range(ny)])]
    ppermute x0 -> x6, starting transfers between devices: none -> 9.01 us  [per_device(): lax.ppermute(x, 'col_0', [(i, (i + d) % ny) for i in range(ny)])]
    div x1 -> x0, other arithmetic: 8.41 us -> none  [per_device(): return galerkin.reshape(AGD, AGD * peers, tile, tile) / (bound + 1e-06)]
    all_to_all x6 -> x3, starting transfers between devices: 27.2 us -> 20 us  [per_device(): lax.all_to_all(x, axis, split_axis=0, concat_axis=0, tiled=True)]
    unnamed x22 -> x32, local copies, waits for them, and re-layouts: 7.46 us -> 1.07 us
    ppermute x8, waiting for transfers between devices: 15.6 us -> 9.88 us  [per_device(): hop = lambda x, way: lax.ppermute(x, 'col_1', around[way])]
  transfers between devices with their start and end apart: 14 -> 17, of which waited for: 5 -> 7; matrix products, arithmetic and copies ran while one was open for 2% -> 4% of each run, Pallas kernels for 52% -> 17%
where the time goes in v2:
time: 132 us; the launch traced here: 131 us
  starting transfers between devices  45.2 us (34%)
  Pallas kernels  40 us (30%)
  waiting for transfers between devices  35 us (27%)
  other arithmetic  5.18 us (4%)
  local copies, waits for them, and re-layouts  4.89 us (4%)
    all_to_all x3, starting transfers between devices, per_device(): lax.all_to_all(x, axis, split_axis=0, concat_axis=0, tiled=True)  20 us
    ppermute x6, waiting for transfers between devices, per_device(): lax.ppermute(x, 'col_0', [(i, (i + d) % ny) for i in range(ny)])  16.6 us
    ppermute x8, starting transfers between devices, per_device(): hop = lambda x, way: lax.ppermute(x, 'col_1', around[way])  16.2 us
    pallas_call x1, Pallas kernels, sum_terms(): pl.pallas_call(terms_kernel, in_specs=[SMEM, ANY] + [ANY] * len(parts), o...  11.9 us
    ppermute x8, waiting for transfers between devices, per_device(): hop = lambda x, way: lax.ppermute(x, 'col_1', around[way])  9.88 us
    pallas_call x3, Pallas kernels, pick(): pl.pallas_call(functools.partial(pick_kernel, steps, apart), in_specs=[SM...  9.67 us
    ppermute x6, starting transfers between devices, per_device(): lax.ppermute(x, 'col_0', [(i, (i + d) % ny) for i in range(ny)])  9.01 us
    all_to_all x3, waiting for transfers between devices, per_device(): lax.all_to_all(x, axis, split_axis=0, concat_axis=0, tiled=True)  8.57 us
  transfers between devices with their start and end apart: 17, of which 7 were waited for; matrix products, arithmetic and copies ran while one was open for 4% of the time, Pallas kernels for 17%

profile of v2, /device:TPU:1, one launch (start us, length us, event | category | flops | bytes accessed | tf_op | source)
XLA Modules:
  0.0 130.7 jit_solution(143151495564627791)
XLA Ops:
  0.0 0.7 fusion.10
  0.7 0.1 broadcast_in_dim.118
  0.8 1.1 pad_maximum_fusion.refs_0_
  1.9 6.5 %collective-permute-start.1 = (f32[8,136,128]{2,1,0:T(8,128)S(1)}, f32[8,136,128]{2,1,0:T(8,128)S(1)}, u32[]{:S(2)}, u32[]{:S(2)}) collective-permute-start(f32[8,136,128]{2,1,0:T(8,128)S(1)} %pad_maximum_fusion.refs_0_), channel_id=1, source_target_pairs={{0,7},{1,0},{2,1},{3,2},{4,3},{5,4},{6,5},{7,6},{8,15},{9,8},{10,9... | collective-permute-start | bytes 1671176 | tf_op jit(solution)/shard_map/ppermute | solution.py:318
  8.4 0.0 collective-permute-start
  8.4 1.5 %fusion.4 = (s32[8,8]{1,0:T(8,128)S(1)}, s32[]{:T(128)}) fusion(s32[8,8]{1,0:T(8,128)} %param.8, s32[8]{0:T(128)} %param.7), kind=kLoop, calls=%fused_computation.25 | loop fusion | flops 255 | bytes 548 | tf_op jit(solution)/shard_map/jit(_where)/select_n | solution.py:324
  9.9 0.6 broadcast_in_dim.113
  10.5 4.2 %all-to-all-start = ((s32[4,8,8]{2,1,0:T(8,128)}), s32[4,8,8]{2,1,0:T(8,128)S(1)}, u32[]{:S(2)}, u32[]{:S(2)}) async-start(s32[4,8,8]{2,1,0:T(8,128)} %broadcast_in_dim.113), calls=%async_computation | async-start | bytes 32768 | tf_op jit(solution)/shard_map/all_to_all | solution.py:319
  14.7 8.2 %inner.1 = (bf16[8,8,256,128]{3,2,1,0:T(8,128)(2,1)}, f32[8,128]{1,0:T(8,128)}) custom-call(f32[8,8,128,128]{3,2,1,0:T(8,128)} %blocks_ref.1, f32[8,128,128]{2,1,0:T(8,128)} %prolong_ref.1), custom_call_target="tpu_custom_call" | custom-call | flops 1073741824 | bytes 9437184 | tf_op jit(solution)/shard_map/inner/pallas_call | solution.py:52
  22.9 0.1 reshape.514
  23.0 0.0 collective-permute-done.1.refs_2_
  23.0 2.8 %collective-permute-start.3 = (f32[8,136,128]{2,1,0:T(8,128)S(1)}, f32[8,136,128]{2,1,0:T(8,128)}, u32[]{:S(2)}, u32[]{:S(2)}) collective-permute-start(f32[8,136,128]{2,1,0:T(8,128)S(1)} %collective-permute-done.1.refs_2_), channel_id=1, source_target_pairs={{0,7},{1,0},{2,1},{3,2},{4,3},{5,4},{6,5},{7,6},{8,15},{9,8},{10,9... | collective-permute-start | bytes 1671176 | tf_op jit(solution)/shard_map/ppermute | solution.py:318
  25.7 0.0 collective-permute-done.refs_1_
  25.7 0.0 collective-permute-start.2
  25.7 0.0 all-to-all-done
  25.8 0.2 select_reduce_fusion.1
  26.0 0.1 copy.16
  26.1 0.6 copy.17.pick_ref
  26.7 0.0 copy-done.1
  26.7 0.0 copy-done.4
  26.7 3.3 %pick.3 = f32[4,6,136,128]{3,2,1,0:T(8,128)} custom-call(s32[4,16]{1,0:T(4,128)} %copy.17.pick_ref, s32[1]{0:T(128)} %bitcast.7.at_ref, f32[8,136,128]{2,1,0:T(8,128)} %copy-done.1, f32[8,136,128]{2,1,0:T(8,128)} %copy-done.4, f32[8,136,128]{2,1,0:T(8,128)} %copy-done.5, f32[8,128]{1,0:T(8,128)} %get-tuple-element.19.refs_3_), custom_call_target="tpu_custom_call" | custom-call | bytes 8388608 | tf_op jit(solution)/shard_map/pick/pallas_call | solution.py:108
  30.0 4.2 %all-to-all-start.1 = ((f32[4,6,136,128]{3,2,1,0:T(8,128)}), f32[4,6,136,128]{3,2,1,0:T(8,128)S(1)}, u32[]{:S(2)}, u32[]{:S(2)}) async-start(f32[4,6,136,128]{3,2,1,0:T(8,128)} %pick.3), calls=%async_computation.1 | async-start | bytes 3342336 | tf_op jit(solution)/shard_map/all_to_all | solution.py:319
  34.3 1.8 %collective-permute-done.3.refs_1_ = f32[8,136,128]{2,1,0:T(8,128)} collective-permute-done((f32[8,136,128]{2,1,0:T(8,128)S(1)}, f32[8,136,128]{2,1,0:T(8,128)}, u32[]{:S(2)}, u32[]{:S(2)}) %collective-permute-start.3) | collective-permute-done | bytes 557088 | tf_op jit(solution)/shard_map/ppermute | solution.py:318
  36.1 3.5 %collective-permute-start.8 = (f32[8,136,128]{2,1,0:T(8,128)}, f32[8,136,128]{2,1,0:T(8,128)S(1)}, u32[]{:S(2)}, u32[]{:S(2)}) collective-permute-start(f32[8,136,128]{2,1,0:T(8,128)} %collective-permute-done.3.refs_1_), channel_id=1, source_target_pairs={{0,7},{1,0},{2,1},{3,2},{4,3},{5,4},{6,5},{7,6},{8,15},{9,8},{10,9... | collective-permute-start | bytes 1671176 | tf_op jit(solution)/shard_map/ppermute | solution.py:318
  39.6 0.0 collective-permute-done.2.refs_0_
  39.6 0.0 collective-permute-start.7
  39.7 0.1 iota_compare_fusion.2
  39.7 0.1 lt.84
  39.8 0.1 broadcast_in_dim.109
  39.9 0.1 mul.150
  40.0 0.2 select_reduce_fusion.4
  40.2 0.3 copy-done.6
  40.5 3.0 %pick.4 = (f32[4,136,128]{2,1,0:T(8,128)}, f32[4,136,128]{2,1,0:T(8,128)}, f32[4,136,128]{2,1,0:T(8,128)}, f32[4,136,128]{2,1,0:T(8,128)}) custom-call(s32[4,16]{1,0:T(4,128)} %copy.17.pick_ref, s32[1]{0:T(128)} %bitcast.7.at_ref, f32[8,136,128]{2,1,0:T(8,128)} %copy-done.6, f32[8,136,128]{2,1,0:T(8,128)} %collective-permute-done.3.refs_1_), custom_call_target="tpu_custom_call" | custom-call | bytes 8388608 | tf_op jit(solution)/shard_map/pick/pallas_call | solution.py:108
  43.5 1.3 collective-permute-start.4
  44.8 4.7 %collective-permute-done.8.refs_1_ = f32[8,136,128]{2,1,0:T(8,128)S(1)} collective-permute-done((f32[8,136,128]{2,1,0:T(8,128)}, f32[8,136,128]{2,1,0:T(8,128)S(1)}, u32[]{:S(2)}, u32[]{:S(2)}) %collective-permute-start.8) | collective-permute-done | bytes 557088 | tf_op jit(solution)/shard_map/ppermute | solution.py:318
  49.5 3.4 %collective-permute-start.10 = (f32[4,136,128]{2,1,0:T(8,128)S(1)}, f32[4,136,128]{2,1,0:T(8,128)S(1)}, u32[]{:S(2)}, u32[]{:S(2)}) collective-permute-start(f32[4,136,128]{2,1,0:T(8,128)S(1)} %slice.9), channel_id=1, source_target_pairs={{0,7},{1,0},{2,1},{3,2},{4,3},{5,4},{6,5},{7,6},{8,15},{9,8},{10,9... | collective-permute-start | bytes 835592 | tf_op jit(solution)/shard_map/ppermute | solution.py:318
  52.8 0.0 collective-permute-done.7.refs_0_
  52.9 0.1 collective-permute-start.9
  53.0 0.1 select_reduce_fusion.5
  53.1 2.5 %collective-permute-start.5 = (f32[4,136,128]{2,1,0:T(8,128)}, f32[4,136,128]{2,1,0:T(8,128)S(1)}, u32[]{:S(2)}, u32[]{:S(2)}) collective-permute-start(f32[4,136,128]{2,1,0:T(8,128)} %get-tuple-element.22), channel_id=1, source_target_pairs={{0,16},{8,24},{16,0},{24,8},{1,17},{9,25},{17,1},{25,9},{2,18},{10... | collective-permute-start | bytes 835592 | tf_op jit(solution)/shard_map/ppermute | solution.py:345
  55.6 0.9 collective-permute-start.6
  56.5 0.0 collective-permute-done.10.refs_3_
  56.5 3.3 %collective-permute-done.9.refs_2_ = f32[4,136,128]{2,1,0:T(8,128)} collective-permute-done((f32[4,136,128]{2,1,0:T(8,128)S(1)}, f32[4,136,128]{2,1,0:T(8,128)}, u32[]{:S(2)}, u32[]{:S(2)}) %collective-permute-start.9) | collective-permute-done | bytes 278560 | tf_op jit(solution)/shard_map/ppermute | solution.py:318
  59.9 3.3 %pick.5 = (f32[6,136,128]{2,1,0:T(8,128)}, f32[6,136,128]{2,1,0:T(8,128)}, f32[6,136,128]{2,1,0:T(8,128)}, f32[6,136,128]{2,1,0:T(8,128)}) custom-call(s32[4,16]{1,0:T(4,128)} %copy.17.pick_ref, s32[1]{0:T(128)} %bitcast.7.at_ref, f32[8,136,128]{2,1,0:T(8,128)} %copy-done.3, f32[8,136,128]{2,1,0:T(8,128)} %copy-done.2, ...), custom_call_target="tpu_custom_call" | custom-call | bytes 8388608 | tf_op jit(solution)/shard_map/pick/pallas_call | solution.py:108
  63.2 0.8 collective-permute-start.11
  64.0 2.4 %collective-permute-start.12 = (f32[6,136,128]{2,1,0:T(8,128)}, f32[6,136,128]{2,1,0:T(8,128)S(1)}, u32[]{:S(2)}, u32[]{:S(2)}) collective-permute-start(f32[6,136,128]{2,1,0:T(8,128)} %get-tuple-element.26), channel_id=1, source_target_pairs={{0,16},{8,24},{16,0},{24,8},{1,17},{9,25},{17,1},{25,9},{2,18},{10... | collective-permute-start | bytes 1253384 | tf_op jit(solution)/shard_map/ppermute | solution.py:345
  66.4 0.0 collective-permute-done.4.refs_2_
  66.4 1.2 collective-permute-start.13
  67.6 0.8 pad.7.clone
  68.3 0.6 add_add_fusion.slot_ref
  69.0 0.0 collective-permute-done.5.refs_3_
  69.0 0.0 collective-permute-done.6.refs_4_
  69.0 0.0 all-to-all-done.1
  69.0 5.5 %collective-permute-done.11.refs_6_ = f32[6,136,128]{2,1,0:T(8,128)S(1)} collective-permute-done((f32[6,136,128]{2,1,0:T(8,128)}, f32[6,136,128]{2,1,0:T(8,128)S(1)}, u32[]{:S(2)}, u32[]{:S(2)}) %collective-permute-start.11) | collective-permute-done | bytes 417824 | tf_op jit(solution)/shard_map/ppermute | solution.py:345
  74.5 6.9 %collective-permute-done.12.refs_7_ = f32[6,136,128]{2,1,0:T(8,128)S(1)} collective-permute-done((f32[6,136,128]{2,1,0:T(8,128)}, f32[6,136,128]{2,1,0:T(8,128)S(1)}, u32[]{:S(2)}, u32[]{:S(2)}) %collective-permute-start.12) | collective-permute-done | bytes 417824 | tf_op jit(solution)/shard_map/ppermute | solution.py:345
  81.4 4.2 %collective-permute-done.13.refs_8_ = f32[6,136,128]{2,1,0:T(8,128)S(1)} collective-permute-done((f32[6,136,128]{2,1,0:T(8,128)}, f32[6,136,128]{2,1,0:T(8,128)S(1)}, u32[]{:S(2)}, u32[]{:S(2)}) %collective-permute-start.13) | collective-permute-done | bytes 417824 | tf_op jit(solution)/shard_map/ppermute | solution.py:345
  85.6 0.7 copy-done.9
  86.3 11.9 %terms.1 = (f32[128,128,128]{2,1,0:T(8,128)}, s32[264]{0:T(512)}, f32[1,128]{1,0:T(1,128)}) custom-call(s32[4,64]{1,0:T(4,128)} %add_add_fusion.slot_ref, bf16[64,256,128]{2,1,0:T(8,128)(2,1)} %bitcast.16, f32[24,136,128]{2,1,0:T(8,128)} %bitcast.15, f32[4,136,128]{2,1,0:T(8,128)} %get-tuple-element.20.refs_1_, f32[4,136,128]{2,1,0:T(8,128)} %copy-done.10, ...), custom_call_target="tpu_custom_call" | custom-call | flops 1073741824 | bytes 16777216 | tf_op jit(solution)/shard_map/terms/pallas_call | solution.py:207
  98.3 1.3 %broadcast_in_dim.119 = f32[256,1,128]{2,1,0:T(1,128)} broadcast(f32[128]{0:T(128)} %bitcast.23), dimensions={2} | broadcast | bytes 131584 | tf_op jit(solution)/shard_map/broadcast_in_dim | solution.py:380
  99.6 11.5 %all-to-all-start.2 = ((f32[256,1,128]{2,1,0:T(1,128)}), f32[256,1,128]{2,1,0:T(1,128)S(1)}, u32[]{:S(2)}, u32[]{:S(2)}) async-start(f32[256,1,128]{2,1,0:T(1,128)} %broadcast_in_dim.119), calls=%async_computation.2 | async-start | bytes 262144 | tf_op jit(solution)/shard_map/all_to_all | solution.py:319
  111.1 4.5 %clear.1._ = f32[128,128,128]{2,1,0:T(8,128)} custom-call(s32[264]{0:T(512)} %get-tuple-element.28.used_ref, f32[128,128,128]{2,1,0:T(8,128)} %get-tuple-element.30._), custom_call_target="tpu_custom_call", output_to_operand_aliasing={{}: (1, {})} | custom-call | bytes 8388608 | tf_op jit(solution)/shard_map/clear/pallas_call | solution.py:253
  115.6 8.6 %all-to-all-done.2 = f32[256,1,128]{2,1,0:T(1,128)S(1)} async-done(((f32[256,1,128]{2,1,0:T(1,128)}), f32[256,1,128]{2,1,0:T(1,128)S(1)}, u32[]{:S(2)}, u32[]{:S(2)}) %all-to-all-start.2) | async-done | bytes 131104 | tf_op jit(solution)/shard_map/all_to_all | solution.py:319
  124.2 0.6 reduce_max.19
  124.8 5.8 %scale.1 = f32[128,128,128]{2,1,0:T(8,128)} custom-call(s32[264]{0:T(512)} %get-tuple-element.28.used_ref, f32[1,1]{1,0:T(1,128)} %bitcast.11.most_ref, f32[128,128,128]{2,1,0:T(8,128)} %clear.1._), custom_call_target="tpu_custom_call", output_to_operand_aliasing={{}: (2, {})} | custom-call | tf_op jit(solution)/shard_map/scale/pallas_call | solution.py:285
  (37 shorter events, 0.2 us)
Async XLA Ops:
  0.0 22.9 %copy-start.14 = (s32[8,8]{1,0:T(8,128)S(1)}, s32[8,8]{1,0:T(8,128)}, u32[]{:S(2)}) copy-start(s32[8,8]{1,0:T(8,128)} %param.8) | copy-start | bytes 772
  1.9 24.8 %copy-start.1 = (f32[8,136,128]{2,1,0:T(8,128)}, f32[8,136,128]{2,1,0:T(8,128)S(1)}, u32[]{:S(2)}) copy-start(f32[8,136,128]{2,1,0:T(8,128)S(1)} %pad_maximum_fusion.refs_0_) | copy-start | bytes 1671172
  1.9 21.1 %collective-permute-start.1 = (f32[8,136,128]{2,1,0:T(8,128)S(1)}, f32[8,136,128]{2,1,0:T(8,128)S(1)}, u32[]{:S(2)}, u32[]{:S(2)}) collective-permute-start(f32[8,136,128]{2,1,0:T(8,128)S(1)} %pad_maximum_fusion.refs_0_), channel_id=1, source_target_pairs={{0,7},{1,0},{2,1},{3,2},{4,3},{5,4},{6,5},{7,6},{8,15},{9,8},{10,9... | collective-permute-start | bytes 1671176 | tf_op jit(solution)/shard_map/ppermute | solution.py:318
  8.4 17.3 %collective-permute-start = (f32[8,136,128]{2,1,0:T(8,128)S(1)}, f32[8,136,128]{2,1,0:T(8,128)S(1)}, u32[]{:S(2)}, u32[]{:S(2)}) collective-permute-start(f32[8,136,128]{2,1,0:T(8,128)S(1)} %pad_maximum_fusion.refs_0_), channel_id=1, source_target_pairs={{0,1},{1,2},{2,3},{3,4},{4,5},{5,6},{6,7},{7,0},{8,9},{9,10},{10,1... | collective-permute-start | bytes 1671176 | tf_op jit(solution)/shard_map/ppermute | solution.py:318
  10.5 15.3 %all-to-all-start = ((s32[4,8,8]{2,1,0:T(8,128)}), s32[4,8,8]{2,1,0:T(8,128)S(1)}, u32[]{:S(2)}, u32[]{:S(2)}) async-start(s32[4,8,8]{2,1,0:T(8,128)} %broadcast_in_dim.113), calls=%async_computation | async-start | bytes 32768 | tf_op jit(solution)/shard_map/all_to_all | solution.py:319
  22.9 16.8 %copy-start.15 = (s32[8]{0:T(128)S(1)}, s32[8]{0:T(128)}, u32[]{:S(2)}) copy-start(s32[8]{0:T(128)} %param.7) | copy-start | bytes 100
  23.0 3.7 %copy-start.5 = (f32[8,136,128]{2,1,0:T(8,128)}, f32[8,136,128]{2,1,0:T(8,128)S(1)}, u32[]{:S(2)}) copy-start(f32[8,136,128]{2,1,0:T(8,128)S(1)} %collective-permute-done.1.refs_2_) | copy-start | bytes 1671172
  23.0 13.2 %collective-permute-start.3 = (f32[8,136,128]{2,1,0:T(8,128)S(1)}, f32[8,136,128]{2,1,0:T(8,128)}, u32[]{:S(2)}, u32[]{:S(2)}) collective-permute-start(f32[8,136,128]{2,1,0:T(8,128)S(1)} %collective-permute-done.1.refs_2_), channel_id=1, source_target_pairs={{0,7},{1,0},{2,1},{3,2},{4,3},{5,4},{6,5},{7,6},{8,15},{9,8},{10,9... | collective-permute-start | bytes 1671176 | tf_op jit(solution)/shard_map/ppermute | solution.py:318
  25.7 1.0 copy-start.4
  25.7 13.9 %collective-permute-start.2 = (f32[8,136,128]{2,1,0:T(8,128)S(1)}, f32[8,136,128]{2,1,0:T(8,128)S(1)}, u32[]{:S(2)}, u32[]{:S(2)}) collective-permute-start(f32[8,136,128]{2,1,0:T(8,128)S(1)} %collective-permute-done.refs_1_), channel_id=1, source_target_pairs={{0,1},{1,2},{2,3},{3,4},{4,5},{5,6},{6,7},{7,0},{8,9},{9,10},{10,1... | collective-permute-start | bytes 1671176 | tf_op jit(solution)/shard_map/ppermute | solution.py:318
  30.0 38.9 %all-to-all-start.1 = ((f32[4,6,136,128]{3,2,1,0:T(8,128)}), f32[4,6,136,128]{3,2,1,0:T(8,128)S(1)}, u32[]{:S(2)}, u32[]{:S(2)}) async-start(f32[4,6,136,128]{3,2,1,0:T(8,128)} %pick.3), calls=%async_computation.1 | async-start | bytes 3342336 | tf_op jit(solution)/shard_map/all_to_all | solution.py:319
  36.1 13.3 %collective-permute-start.8 = (f32[8,136,128]{2,1,0:T(8,128)}, f32[8,136,128]{2,1,0:T(8,128)S(1)}, u32[]{:S(2)}, u32[]{:S(2)}) collective-permute-start(f32[8,136,128]{2,1,0:T(8,128)} %collective-permute-done.3.refs_1_), channel_id=1, source_target_pairs={{0,7},{1,0},{2,1},{3,2},{4,3},{5,4},{6,5},{7,6},{8,15},{9,8},{10,9... | collective-permute-start | bytes 1671176 | tf_op jit(solution)/shard_map/ppermute | solution.py:318
  39.6 0.8 copy-start.6
  39.6 13.2 %collective-permute-start.7 = (f32[8,136,128]{2,1,0:T(8,128)S(1)}, f32[8,136,128]{2,1,0:T(8,128)S(1)}, u32[]{:S(2)}, u32[]{:S(2)}) collective-permute-start(f32[8,136,128]{2,1,0:T(8,128)S(1)} %collective-permute-done.2.refs_0_), channel_id=1, source_target_pairs={{0,1},{1,2},{2,3},{3,4},{4,5},{5,6},{6,7},{7,0},{8,9},{9,10},{10,1... | collective-permute-start | bytes 1671176 | tf_op jit(solution)/shard_map/ppermute | solution.py:318
  43.5 22.9 %collective-permute-start.4 = (f32[4,136,128]{2,1,0:T(8,128)}, f32[4,136,128]{2,1,0:T(8,128)S(1)}, u32[]{:S(2)}, u32[]{:S(2)}) collective-permute-start(f32[4,136,128]{2,1,0:T(8,128)} %get-tuple-element.21), channel_id=1, source_target_pairs={{0,8},{8,16},{16,24},{24,0},{1,9},{9,17},{17,25},{25,1},{2,10},{10... | collective-permute-start | bytes 835592 | tf_op jit(solution)/shard_map/ppermute | solution.py:345
  49.4 10.4 %copy-start.2 = (f32[8,136,128]{2,1,0:T(8,128)}, f32[8,136,128]{2,1,0:T(8,128)S(1)}, u32[]{:S(2)}) copy-start(f32[8,136,128]{2,1,0:T(8,128)S(1)} %collective-permute-done.8.refs_1_) | copy-start | bytes 1671172
  49.5 7.0 %collective-permute-start.10 = (f32[4,136,128]{2,1,0:T(8,128)S(1)}, f32[4,136,128]{2,1,0:T(8,128)S(1)}, u32[]{:S(2)}, u32[]{:S(2)}) collective-permute-start(f32[4,136,128]{2,1,0:T(8,128)S(1)} %slice.9), channel_id=1, source_target_pairs={{0,7},{1,0},{2,1},{3,2},{4,3},{5,4},{6,5},{7,6},{8,15},{9,8},{10,9... | collective-permute-start | bytes 835592 | tf_op jit(solution)/shard_map/ppermute | solution.py:318
  52.8 7.0 %copy-start.3 = (f32[8,136,128]{2,1,0:T(8,128)}, f32[8,136,128]{2,1,0:T(8,128)S(1)}, u32[]{:S(2)}) copy-start(f32[8,136,128]{2,1,0:T(8,128)S(1)} %collective-permute-done.7.refs_0_) | copy-start | bytes 1671172
  52.9 7.0 %collective-permute-start.9 = (f32[4,136,128]{2,1,0:T(8,128)S(1)}, f32[4,136,128]{2,1,0:T(8,128)}, u32[]{:S(2)}, u32[]{:S(2)}) collective-permute-start(f32[4,136,128]{2,1,0:T(8,128)S(1)} %slice.8), channel_id=1, source_target_pairs={{0,1},{1,2},{2,3},{3,4},{4,5},{5,6},{6,7},{7,0},{8,9},{9,10},{10,1... | collective-permute-start | bytes 835592 | tf_op jit(solution)/shard_map/ppermute | solution.py:318
  53.1 15.8 %collective-permute-start.5 = (f32[4,136,128]{2,1,0:T(8,128)}, f32[4,136,128]{2,1,0:T(8,128)S(1)}, u32[]{:S(2)}, u32[]{:S(2)}) collective-permute-start(f32[4,136,128]{2,1,0:T(8,128)} %get-tuple-element.22), channel_id=1, source_target_pairs={{0,16},{8,24},{16,0},{24,8},{1,17},{9,25},{17,1},{25,9},{2,18},{10... | collective-permute-start | bytes 835592 | tf_op jit(solution)/shard_map/ppermute | solution.py:345
  55.6 13.4 %collective-permute-start.6 = (f32[4,136,128]{2,1,0:T(8,128)}, f32[4,136,128]{2,1,0:T(8,128)S(1)}, u32[]{:S(2)}, u32[]{:S(2)}) collective-permute-start(f32[4,136,128]{2,1,0:T(8,128)} %get-tuple-element.23), channel_id=1, source_target_pairs={{0,24},{8,0},{16,8},{24,16},{1,25},{9,1},{17,9},{25,17},{2,26},{10... | collective-permute-start | bytes 835592 | tf_op jit(solution)/shard_map/ppermute | solution.py:345
  56.5 3.4 %copy-start.13 = (f32[4,136,128]{2,1,0:T(8,128)}, f32[4,136,128]{2,1,0:T(8,128)S(1)}, u32[]{:S(2)}) copy-start(f32[4,136,128]{2,1,0:T(8,128)S(1)} %collective-permute-done.10.refs_3_) | copy-start | bytes 835588
  63.2 11.3 %collective-permute-start.11 = (f32[6,136,128]{2,1,0:T(8,128)}, f32[6,136,128]{2,1,0:T(8,128)S(1)}, u32[]{:S(2)}, u32[]{:S(2)}) collective-permute-start(f32[6,136,128]{2,1,0:T(8,128)} %get-tuple-element.25), channel_id=1, source_target_pairs={{0,8},{8,16},{16,24},{24,0},{1,9},{9,17},{17,25},{25,1},{2,10},{10... | collective-permute-start | bytes 1253384 | tf_op jit(solution)/shard_map/ppermute | solution.py:345
  64.0 17.4 %collective-permute-start.12 = (f32[6,136,128]{2,1,0:T(8,128)}, f32[6,136,128]{2,1,0:T(8,128)S(1)}, u32[]{:S(2)}, u32[]{:S(2)}) collective-permute-start(f32[6,136,128]{2,1,0:T(8,128)} %get-tuple-element.26), channel_id=1, source_target_pairs={{0,16},{8,24},{16,0},{24,8},{1,17},{9,25},{17,1},{25,9},{2,18},{10... | collective-permute-start | bytes 1253384 | tf_op jit(solution)/shard_map/ppermute | solution.py:345
  66.4 2.6 %copy-start.10 = (f32[4,136,128]{2,1,0:T(8,128)}, f32[4,136,128]{2,1,0:T(8,128)S(1)}, u32[]{:S(2)}) copy-start(f32[4,136,128]{2,1,0:T(8,128)S(1)} %collective-permute-done.4.refs_2_) | copy-start | bytes 835588
  66.4 19.2 %collective-permute-start.13 = (f32[6,136,128]{2,1,0:T(8,128)}, f32[6,136,128]{2,1,0:T(8,128)S(1)}, u32[]{:S(2)}, u32[]{:S(2)}) collective-permute-start(f32[6,136,128]{2,1,0:T(8,128)} %get-tuple-element.27), channel_id=1, source_target_pairs={{0,24},{8,0},{16,8},{24,16},{1,25},{9,1},{17,9},{25,17},{2,26},{10... | collective-permute-start | bytes 1253384 | tf_op jit(solution)/shard_map/ppermute | solution.py:345
  69.0 16.6 %copy-start.11 = (f32[4,136,128]{2,1,0:T(8,128)}, f32[4,136,128]{2,1,0:T(8,128)S(1)}, u32[]{:S(2)}) copy-start(f32[4,136,128]{2,1,0:T(8,128)S(1)} %collective-permute-done.5.refs_3_) | copy-start | bytes 835588
  69.0 16.6 %copy-start.12 = (f32[4,136,128]{2,1,0:T(8,128)}, f32[4,136,128]{2,1,0:T(8,128)S(1)}, u32[]{:S(2)}) copy-start(f32[4,136,128]{2,1,0:T(8,128)S(1)} %collective-permute-done.6.refs_4_) | copy-start | bytes 835588
  69.0 16.6 %copy-start = (f32[4,6,136,128]{3,2,1,0:T(8,128)}, f32[4,6,136,128]{3,2,1,0:T(8,128)S(1)}, u32[]{:S(2)}) copy-start(f32[4,6,136,128]{3,2,1,0:T(8,128)S(1)} %all-to-all-done.1) | copy-start | bytes 5013508
  74.5 11.1 %copy-start.7 = (f32[6,136,128]{2,1,0:T(8,128)}, f32[6,136,128]{2,1,0:T(8,128)S(1)}, u32[]{:S(2)}) copy-start(f32[6,136,128]{2,1,0:T(8,128)S(1)} %collective-permute-done.11.refs_6_) | copy-start | bytes 1253380
  81.4 4.2 %copy-start.8 = (f32[6,136,128]{2,1,0:T(8,128)}, f32[6,136,128]{2,1,0:T(8,128)S(1)}, u32[]{:S(2)}) copy-start(f32[6,136,128]{2,1,0:T(8,128)S(1)} %collective-permute-done.12.refs_7_) | copy-start | bytes 1253380
  85.6 0.8 copy-start.9
  99.6 24.6 %all-to-all-start.2 = ((f32[256,1,128]{2,1,0:T(1,128)}), f32[256,1,128]{2,1,0:T(1,128)S(1)}, u32[]{:S(2)}, u32[]{:S(2)}) async-start(f32[256,1,128]{2,1,0:T(1,128)} %broadcast_in_dim.119), calls=%async_computation.2 | async-start | bytes 262144 | tf_op jit(solution)/shard_map/all_to_all | solution.py:319

commit v3 on v2

--- a/solution.py
+++ b/solution.py
@@ -18,9 +18,9 @@
 HBM = pl.BlockSpec(memory_space=pltpu.HBM)
 MIB = 1 << 20
 UNROLL = 4
+CHUNK = 8
 CUTS = (1,2)
 MERGED = 1
-EARLY = 0
 LIMIT = 60
 
 
@@ -120,12 +120,39 @@
     )(picks, at, *sets, *after)
 
 
-def terms_kernel(slot_ref, inner_ref, *refs):
-    parts, rest = refs[:-13], refs[-13:]
-    out_ref, used_ref, most_ref, left, held, right, sums, most, ids, agg_ref, sem, sems, part_sems = rest
-    wide = out_ref.shape[0]
-    tile = out_ref.shape[-1]
-    load = pltpu.make_async_copy(inner_ref, left, sem)
+def terms_kernel(first, final, parts_n, slot_ref, inner_ref, *refs):
+    parts = refs[:parts_n]
+    if final:
+        old_ref, old_tiles = refs[parts_n : parts_n + 2]
+        outs = refs[parts_n + 2 : parts_n + 5]
+        most_ref = outs[2]
+    else:
+        outs = refs[parts_n : parts_n + 2]
+    out_ref, used_ref = outs[:2]
+    left, held, right, sums, most, ids, agg_ref, sem, sems, part_sems, left_sems = refs[-11:]
+    wide = used_ref.shape[0] // 2 - 4
+    spare, tile = out_ref.shape[0], out_ref.shape[-1]
+    begin = slot_ref[3, 0] if final else 0
+    end = begin + slot_ref[3, 1] if final else slot_ref[3, 0]
+
+    def load(s):
+        return pltpu.make_async_copy(inner_ref.at[slot_ref[0, s]], left.at[s], left_sems.at[s])
+
+    def save(n):
+        at = pl.ds(CHUNK * n, CHUNK)
+        return pltpu.make_async_copy(sums.at[at], out_ref.at[at], sems.at[n])
+
+    def back(n):
+        at = pl.ds(CHUNK * n, CHUNK)
+        return pltpu.make_async_copy(old_tiles.at[at], sums.at[at], sems.at[n])
+
+    def loads(do):
+        def step(s, _):
+            do(load(s))
+            return 0
+
+        lax.fori_loop(begin, end, step, 0)
+
     copies = []
     at = 0
     for n, part in enumerate(parts):
@@ -133,107 +160,121 @@
         copies.append(pltpu.make_async_copy(part, held.at[pl.ds(at, count)], part_sems.at[n]))
         copies[-1].start()
         at += count
-    load.start()
-
-    def clear(e, _):
+    loads(lambda copy: copy.start())
+
+    def fresh(e, _):
         for n in range(8):
-            used_ref[8 * e + n] = 0
+            used_ref[8 * e + n] = old_ref[8 * e + n] if final else 0
         return 0
 
-    lax.fori_loop(0, used_ref.shape[0] // 8, clear, 0)
-    at = 0
-    for part, copy in zip(parts, copies):
+    lax.fori_loop(0, used_ref.shape[0] // 8, fresh, 0)
+    if final:
+        each_chunk(used_ref, lambda n: back(n).start())
+    for copy in copies:
         copy.wait()
-        for n in range(at, at + part.shape[0]):
-            right[n] = split(held[n, :tile], 1)
-            ids[n : n + 1] = held[n, tile : tile + 1].astype(jnp.int32)
-        at += part.shape[0]
-    load.wait()
+    for n in range(at):
+        ids[n : n + 1] = held[n, tile : tile + 1].astype(jnp.int32)
     look_up = pltpu.make_async_copy(ids, agg_ref, sem)
     look_up.start()
+    for n in range(at):
+        right[n] = split(held[n, :tile], 1)
+    loads(lambda copy: copy.wait())
     look_up.wait()
-    live = slot_ref[3, 0]
+    if final:
+        each_chunk(used_ref, lambda n: back(n).wait())
 
     def some(n, _):
-        terms = []
+        terms, places = [], []
         for m in range(UNROLL):
-            s = UNROLL * n + m
-            terms.append(dot_split(left[slot_ref[0, s]], right[slot_ref[1, s]]))
-        for m in range(UNROLL):
-            s = UNROLL * n + m
-            e = jnp.where(s < live, slot_ref[2, s] + agg_ref[slot_ref[1, s], 0], wide)
-
-            @pl.when(e < wide)
+            s = begin + UNROLL * n + m
+            inside = s < end
+            s = jnp.where(inside, s, begin)
+            source = jnp.clip(slot_ref[1, s] - first, 0, at - 1)
+            places.append(jnp.where(inside, slot_ref[2, s] + agg_ref[source, 0], wide))
+            terms.append(dot_split(left[s], right[source]))
+        for e, term in zip(places, terms):
+
+            @pl.when((e < wide) & (used_ref[jnp.minimum(e, wide - 1)] == 0))
             def _():
-                @pl.when(used_ref[e] == 0)
-                def _():
-                    count = used_ref[2 * wide]
-                    used_ref[e] = 1
-                    used_ref[wide + count] = e
-                    used_ref[2 * wide] = count + 1
-                    sums[e] = jnp.zeros((tile, tile), jnp.float32)
-
-            sums[e] = sums[e] + terms[m]
+                count = used_ref[2 * wide]
+                used_ref[wide + count] = e
+                used_ref[2 * wide] = count + 1
+                used_ref[e] = count + 1
+                sums[count] = jnp.zeros((tile, tile), jnp.float32)
+
+            n = jnp.where(e < wide, used_ref[jnp.minimum(e, wide - 1)] - 1, spare)
+            sums[n] = sums[n] + term
         return 0
 
-    sums[wide] = jnp.zeros((tile, tile), jnp.float32)
-    lax.fori_loop(0, (live + UNROLL - 1) // UNROLL, some, 0)
-    most[...] = jnp.zeros_like(most)
-    half = wide // AGD
-    copy = lambda e: pltpu.make_async_copy(sums.at[e], out_ref.at[e], sems.at[e])
-
-    def look(e):
-        copy(e).start()
-        most[e // half] = most[e // half] + jnp.abs(sums[e])
-
-    each_used(used_ref, look)
-    row_sums = jnp.sum(most[...], axis=2)
-    most_ref[...] = jnp.full(most_ref.shape, jnp.max(row_sums), jnp.float32)
-    each_used(used_ref, lambda e: copy(e).wait())
+    sums[spare] = jnp.zeros((tile, tile), jnp.float32)
+    lax.fori_loop(0, (end - begin + UNROLL - 1) // UNROLL, some, 0)
+    each_chunk(used_ref, lambda n: save(n).start())
+    if final:
+        most[...] = jnp.zeros_like(most)
+        half = wide // AGD
+
+        def look(n, e):
+            most[e // half] = most[e // half] + jnp.abs(sums[n])
+
+        each_used(used_ref, look)
+        row_sums = jnp.sum(most[...], axis=2)
+        most_ref[...] = jnp.full(most_ref.shape, jnp.max(row_sums), jnp.float32)
+    each_chunk(used_ref, lambda n: save(n).wait())
 
 
 def each_used(used_ref, do):
     wide = used_ref.shape[0] // 2 - 4
 
     def step(n, _):
-        do(used_ref[wide + n])
+        do(n, used_ref[wide + n])
         return 0
 
     lax.fori_loop(0, used_ref[2 * wide], step, 0)
 
 
-def sum_terms(slots, inner, parts, wide):
+def each_chunk(used_ref, do):
+    def step(n, _):
+        do(n)
+        return 0
+
+    lax.fori_loop(0, (used_ref[used_ref.shape[0] - 8] + CHUNK - 1) // CHUNK, step, 0)
+
+
+def sum_terms(slots, inner, parts, first, wide, everyone, before=()):
     flat, _, tile = inner.shape
+    final = len(before) > 0
+    count = sum(p.shape[0] for p in parts)
     return pl.pallas_call(
-        terms_kernel,
-        in_specs=[SMEM, ANY] + [ANY] * len(parts),
-        out_specs=[ANY, SMEM, VMEM],
+        functools.partial(terms_kernel, first, final, len(parts)),
+        in_specs=[SMEM, ANY] + [ANY] * len(parts) + [SMEM, ANY] * final,
+        out_specs=[ANY, SMEM] + [VMEM] * final,
         out_shape=[
-            pltpu.HBM((wide, tile, tile), jnp.float32),
+            pltpu.HBM(inner.shape[:1] + (tile, tile), jnp.float32),
             jax.ShapeDtypeStruct((2 * wide + 8,), jnp.int32),
-            jax.ShapeDtypeStruct((1, tile), jnp.float32),
-        ],
+        ]
+        + [jax.ShapeDtypeStruct((everyone, 1, tile), jnp.float32)] * final,
         scratch_shapes=[
             pltpu.VMEM(inner.shape, jnp.bfloat16),
-            pltpu.VMEM((flat, *parts[0].shape[1:]), jnp.float32),
-            pltpu.VMEM((flat, tile, 2 * tile), jnp.bfloat16),
-            pltpu.VMEM((wide + 1, tile, tile), jnp.float32),
+            pltpu.VMEM((count, *parts[0].shape[1:]), jnp.float32),
+            pltpu.VMEM((count, tile, 2 * tile), jnp.bfloat16),
+            pltpu.VMEM((flat + 1, tile, tile), jnp.float32),
             pltpu.VMEM((AGD, tile, tile), jnp.float32),
-            pltpu.VMEM((flat, tile), jnp.int32),
-            pltpu.SMEM((flat, tile), jnp.int32),
+            pltpu.VMEM((count, tile), jnp.int32),
+            pltpu.SMEM((count, tile), jnp.int32),
             pltpu.SemaphoreType.DMA,
-            pltpu.SemaphoreType.DMA((wide,)),
+            pltpu.SemaphoreType.DMA((flat // CHUNK,)),
             pltpu.SemaphoreType.DMA((len(parts),)),
+            pltpu.SemaphoreType.DMA((flat,)),
         ],
         cost_estimate=pl.CostEstimate(
             flops=8 * flat * tile**3, bytes_accessed=16 * MIB, transcendentals=0
         ),
         compiler_params=params(LIMIT),
         name="terms",
-    )(slots, inner, *parts)
-
-
-def clear_kernel(used_ref, _, out_ref, zero, sems):
+    )(slots, inner, *parts, *before)
+
+
+def clear_kernel(used_ref, out_ref, zero, sems):
     zero[...] = jnp.zeros_like(zero)
     copy = lambda e: pltpu.make_async_copy(zero, out_ref.at[e], sems.at[e])
 
@@ -248,54 +289,55 @@
     each(lambda e: copy(e).wait())
 
 
-def clear_rest(used, tiles):
-    wide, tile, _ = tiles.shape
+def clear_rest(used, wide, tile):
     return pl.pallas_call(
         clear_kernel,
-        in_specs=[SMEM, ANY],
+        in_specs=[SMEM],
         out_specs=ANY,
-        out_shape=pltpu.HBM(tiles.shape, jnp.float32),
+        out_shape=pltpu.HBM((wide, tile, tile), jnp.float32),
         scratch_shapes=[
             pltpu.VMEM((tile, tile), jnp.float32),
             pltpu.SemaphoreType.DMA((wide,)),
         ],
-        input_output_aliases={1: 0},
         cost_estimate=pl.CostEstimate(flops=0, bytes_accessed=8 * MIB, transcendentals=0),
         compiler_params=params(LIMIT),
         name="clear",
-    )(used, tiles)
-
-
-def scale_kernel(used_ref, most_ref, _, out_ref, held, come, go):
-    get = lambda e: pltpu.make_async_copy(out_ref.at[e], held.at[e], come.at[e])
-    put = lambda e: pltpu.make_async_copy(held.at[e], out_ref.at[e], go.at[e])
-    factor = 1.0 / (most_ref[0, 0] + 1e-06)
-
-    def one(e):
-        get(e).wait()
-        held[e] = held[e] * factor
-        put(e).start()
-
-    each_used(used_ref, lambda e: get(e).start())
+    )(used)
+
+
+def scale_kernel(used_ref, most_ref, tiles_ref, _, out_ref, held, come, go):
+    def get(n):
+        at = pl.ds(CHUNK * n, CHUNK)
+        return pltpu.make_async_copy(tiles_ref.at[at], held.at[at], come.at[n])
+
+    put = lambda n, e: pltpu.make_async_copy(held.at[n], out_ref.at[e], go.at[n])
+    each_chunk(used_ref, lambda n: get(n).start())
+    factor = 1.0 / (jnp.max(most_ref[...]) + 1e-06)
+
+    def one(n, e):
+        pl.when(n % CHUNK == 0)(lambda: get(n // CHUNK).wait())
+        held[n] = held[n] * factor
+        put(n, e).start()
+
     each_used(used_ref, one)
-    each_used(used_ref, lambda e: put(e).wait())
-
-
-def scale(used, bound, tiles):
+    each_used(used_ref, lambda n, e: put(n, e).wait())
+
+
+def scale(used, bound, tiles, cleared):
     return pl.pallas_call(
         scale_kernel,
-        in_specs=[SMEM, SMEM, ANY],
+        in_specs=[SMEM, VMEM, ANY, ANY],
         out_specs=ANY,
-        out_shape=pltpu.HBM(tiles.shape, jnp.float32),
+        out_shape=pltpu.HBM(cleared.shape, jnp.float32),
         scratch_shapes=[
             pltpu.VMEM(tiles.shape, jnp.float32),
+            pltpu.SemaphoreType.DMA((tiles.shape[0] // CHUNK,)),
             pltpu.SemaphoreType.DMA((tiles.shape[0],)),
-            pltpu.SemaphoreType.DMA((tiles.shape[0],)),
-        ],
-        input_output_aliases={2: 0},
+        ],
+        input_output_aliases={3: 0},
         compiler_params=params(LIMIT),
         name="scale",
-    )(used, bound, tiles)
+    )(used, bound, tiles, cleared)
 
 
 def wanted_ends(cols, owners, rows):
@@ -346,7 +388,8 @@
     for n, steps in enumerate(orders):
         last = nz // 2 in steps
         sets = [held[d] for d in steps if d in held] + ([up, down] if last else [])
-        sent = pick(picks, at, sets, tuple(steps + steps[-1:] * last), n >= MERGED, (done,) * (n == EARLY))
+        after = (done,) if n == 0 else (parts[-1],) * last
+        sent = pick(picks, at, sets, tuple(steps + steps[-1:] * last), n >= MERGED, after)
         if n >= MERGED:
             parts += [sent[0]] + [onward(sent[d], d) for d in range(1, ny)]
         else:
@@ -368,18 +411,25 @@
     row_agg = jnp.broadcast_to(aggregates[:, None], (rows, slots)).reshape(1, flat)
     target = row_agg * wide + owner * AGD
     number = jnp.arange(flat, dtype=jnp.int32)[None, :]
-    place = jnp.sum(jnp.where((number < number.T) & live, 1, 0), axis=1)[:, None]
+    late_from = flat - len(orders[-1]) * ny * CAP
+    early = live & (source < late_from)
+    late = live & (source >= late_from)
+    count = lambda x: jnp.sum(jnp.where((number < number.T) & x, 1, 0), axis=1)[:, None]
+    early_total, late_total = (jnp.sum(x.astype(jnp.int32)) for x in (early, late))
+    place = jnp.where(early.T, count(early), early_total + count(late))
     moved = (place == number) & live.T
-    front = lambda x, rest: jnp.sum(jnp.where(moved, x.T - rest, 0), axis=0)[None, :] + rest
-    total = jnp.broadcast_to(jnp.sum(live.astype(jnp.int32)), (1, flat))
-    where = jnp.concatenate(
-        [front(number, 0), front(source, 0), front(target, AGD * wide), total], axis=0
-    ).astype(jnp.int32)
-    tiles, used, most = sum_terms(where, inner, parts, AGD * wide)
+    front = lambda x: jnp.sum(jnp.where(moved, x.T, 0), axis=0)[None, :]
+    totals = jnp.where(number == 0, early_total, late_total)
+    where = jnp.concatenate([front(number), front(source), front(target), totals], axis=0)
+    where = where.astype(jnp.int32)
     everyone = lax.axis_size(ROW_COL)
-    all_most = swap(jnp.broadcast_to(most, (everyone, tile)), ROW_COL)
-    bound = jnp.max(all_most).reshape(1, 1)
-    return scale(used, bound, clear_rest(used, tiles)).reshape(AGD, wide, tile, tile)
+    add = functools.partial(sum_terms, where, inner, wide=AGD * wide, everyone=everyone)
+    at = len(parts) - ny
+    tiles, used = add(parts[:at], 0)
+    tiles, used, most = add(parts[at:], late_from, before=(used, tiles))
+    all_most = swap(most, ROW_COL)
+    cleared = clear_rest(used, AGD * wide, tile)
+    return scale(used, all_most, tiles, cleared).reshape(AGD, wide, tile, tile)
 
 
 def solution(mesh):

time: 132 us -> 125 us (0.947)
  waiting for transfers between devices: 35 us -> 21.7 us
  Pallas kernels: 40 us -> 42 us
  other arithmetic: 5.18 us -> 7.08 us
  starting transfers between devices: 45.2 us -> 46.7 us
    ppermute x6, waiting for transfers between devices: 16.6 us -> 6.77 us  [per_device(): lax.ppermute(x, 'col_0', [(i, (i + d) % ny) for i in range(ny)])]
    ppermute x8, waiting for transfers between devices: 9.88 us -> 6.35 us  [per_device(): hop = lambda x, way: lax.ppermute(x, 'col_1', around[way])]
    unnamed x32, local copies, waits for them, and re-layouts: 1.07 us -> 3.59 us
    ppermute x6, starting transfers between devices: 9.01 us -> 11.5 us  [per_device(): lax.ppermute(x, 'col_0', [(i, (i + d) % ny) for i in range(ny)])]
    pallas_call x3 -> x4, Pallas kernels: 22.2 us -> 24 us  [the longest x2 15.7 us: sum_terms(): pl.pallas_call(functools.partial(terms_kernel, first, final, len(parts)),...]
    select_n x1 -> x2, other arithmetic: 0.03 us -> 1.74 us  [the longest x1 1.18 us: per_device(): totals = jnp.where(number == 0, early_total, late_total)]
  transfers between devices with their start and end apart: 17 -> 17, of which waited for: 7 -> 6; matrix products, arithmetic and copies ran while one was open for 4% -> 6% of each run, Pallas kernels for 17% -> 25%
where the time goes in v3:
time: 125 us; the launch traced here: 124 us
  starting transfers between devices  46.7 us (37%)
  Pallas kernels  42 us (34%)
  waiting for transfers between devices  21.7 us (17%)
  other arithmetic  7.08 us (6%)
  local copies, waits for them, and re-layouts  6.14 us (5%)
    all_to_all x3, starting transfers between devices, per_device(): lax.all_to_all(x, axis, split_axis=0, concat_axis=0, tiled=True)  18.9 us
    ppermute x8, starting transfers between devices, per_device(): hop = lambda x, way: lax.ppermute(x, 'col_1', around[way])  16.2 us
    pallas_call x2, Pallas kernels, sum_terms(): pl.pallas_call(functools.partial(terms_kernel, first, final, len(parts)),...  15.7 us
    ppermute x6, starting transfers between devices, per_device(): lax.ppermute(x, 'col_0', [(i, (i + d) % ny) for i in range(ny)])  11.5 us
    pallas_call x3, Pallas kernels, pick(): pl.pallas_call(functools.partial(pick_kernel, steps, apart), in_specs=[SM...  9.73 us
    all_to_all x3, waiting for transfers between devices, per_device(): lax.all_to_all(x, axis, split_axis=0, concat_axis=0, tiled=True)  8.61 us
    pallas_call x1, Pallas kernels, inner_products(): pl.pallas_call(inner_kernel, grid=(rows,), in_specs=[pl.BlockSpec((1, slo...  8.22 us
    ppermute x6, waiting for transfers between devices, per_device(): lax.ppermute(x, 'col_0', [(i, (i + d) % ny) for i in range(ny)])  6.77 us
  transfers between devices with their start and end apart: 17, of which 6 were waited for; matrix products, arithmetic and copies ran while one was open for 6% of the time, Pallas kernels for 25%

profile of v3, /device:TPU:1, one launch (start us, length us, event | category | flops | bytes accessed | tf_op | source)
XLA Modules:
  0.0 124.0 jit_solution(15562488677097122106)
XLA Ops:
  0.0 0.7 fusion.27
  0.7 0.1 broadcast_in_dim.122
  0.8 1.1 pad_maximum_fusion.refs_0_
  1.9 6.5 %collective-permute-start.3 = (f32[8,136,128]{2,1,0:T(8,128)S(1)}, f32[8,136,128]{2,1,0:T(8,128)S(1)}, u32[]{:S(2)}, u32[]{:S(2)}) collective-permute-start(f32[8,136,128]{2,1,0:T(8,128)S(1)} %pad_maximum_fusion.refs_0_), channel_id=1, source_target_pairs={{0,7},{1,0},{2,1},{3,2},{4,3},{5,4},{6,5},{7,6},{8,15},{9,8},{10,9... | collective-permute-start | bytes 1671176 | tf_op jit(solution)/shard_map/ppermute | solution.py:360
  8.4 0.0 collective-permute-start
  8.4 0.8 reshape.737
  9.2 0.1 broadcast_in_dim.112
  9.2 0.1 mul.349
  9.3 0.7 iota_compare_fusion.2
  10.1 0.1 lt.132
  10.1 0.2 select_reduce_fusion.7
  10.3 0.1 reduce_min.21
  10.4 0.8 fusion.21
  11.2 0.6 broadcast_in_dim.117
  11.8 4.2 %all-to-all-start = ((s32[4,8,8]{2,1,0:T(8,128)}), s32[4,8,8]{2,1,0:T(8,128)S(1)}, u32[]{:S(2)}, u32[]{:S(2)}) async-start(s32[4,8,8]{2,1,0:T(8,128)} %broadcast_in_dim.117), calls=%async_computation | async-start | bytes 32768 | tf_op jit(solution)/shard_map/all_to_all | solution.py:361
  16.0 8.2 %inner.1 = (bf16[8,8,256,128]{3,2,1,0:T(8,128)(2,1)}, f32[8,128]{1,0:T(8,128)}) custom-call(f32[8,8,128,128]{3,2,1,0:T(8,128)} %blocks_ref.1, f32[8,128,128]{2,1,0:T(8,128)} %prolong_ref.1), custom_call_target="tpu_custom_call" | custom-call | flops 1073741824 | bytes 9437184 | tf_op jit(solution)/shard_map/inner/pallas_call | solution.py:52
  24.2 2.8 %collective-permute-start.4 = (f32[8,136,128]{2,1,0:T(8,128)S(1)}, f32[8,136,128]{2,1,0:T(8,128)}, u32[]{:S(2)}, u32[]{:S(2)}) collective-permute-start(f32[8,136,128]{2,1,0:T(8,128)S(1)} %collective-permute-done.3.refs_2_), channel_id=1, source_target_pairs={{0,7},{1,0},{2,1},{3,2},{4,3},{5,4},{6,5},{7,6},{8,15},{9,8},{10,9... | collective-permute-start | bytes 1671176 | tf_op jit(solution)/shard_map/ppermute | solution.py:360
  27.0 0.0 collective-permute-start.1
  27.0 0.0 all-to-all-done
  27.0 0.2 select_reduce_fusion.1
  27.2 0.1 copy.11
  27.3 0.7 copy.13.pick_ref
  28.0 3.5 %pick.5 = f32[4,6,136,128]{3,2,1,0:T(8,128)} custom-call(s32[4,16]{1,0:T(4,128)} %copy.13.pick_ref, s32[1]{0:T(128)} %bitcast.7.at_ref, f32[8,136,128]{2,1,0:T(8,128)} %copy-done.1, f32[8,136,128]{2,1,0:T(8,128)} %copy-done.5, f32[8,136,128]{2,1,0:T(8,128)} %copy-done.6, f32[8,128]{1,0:T(8,128)} %get-tuple-element.26.refs_3_), custom_call_target="tpu_custom_call" | custom-call | bytes 8388608 | tf_op jit(solution)/shard_map/pick/pallas_call | solution.py:108
  31.5 4.2 %all-to-all-start.1 = ((f32[4,6,136,128]{3,2,1,0:T(8,128)}), f32[4,6,136,128]{3,2,1,0:T(8,128)S(1)}, u32[]{:S(2)}, u32[]{:S(2)}) async-start(f32[4,6,136,128]{3,2,1,0:T(8,128)} %pick.5), calls=%async_computation.1 | async-start | bytes 3342336 | tf_op jit(solution)/shard_map/all_to_all | solution.py:361
  35.7 1.6 %collective-permute-done.4.refs_1_ = f32[8,136,128]{2,1,0:T(8,128)} collective-permute-done((f32[8,136,128]{2,1,0:T(8,128)S(1)}, f32[8,136,128]{2,1,0:T(8,128)}, u32[]{:S(2)}, u32[]{:S(2)}) %collective-permute-start.4) | collective-permute-done | bytes 557088 | tf_op jit(solution)/shard_map/ppermute | solution.py:360
  37.4 3.5 %collective-permute-start.5 = (f32[8,136,128]{2,1,0:T(8,128)}, f32[8,136,128]{2,1,0:T(8,128)S(1)}, u32[]{:S(2)}, u32[]{:S(2)}) collective-permute-start(f32[8,136,128]{2,1,0:T(8,128)} %collective-permute-done.4.refs_1_), channel_id=1, source_target_pairs={{0,7},{1,0},{2,1},{3,2},{4,3},{5,4},{6,5},{7,6},{8,15},{9,8},{10,9... | collective-permute-start | bytes 1671176 | tf_op jit(solution)/shard_map/ppermute | solution.py:360
  40.9 0.1 select_reduce_fusion.5
  41.0 0.7 copy-done.7
  41.7 2.9 %pick.3 = (f32[4,136,128]{2,1,0:T(8,128)}, f32[4,136,128]{2,1,0:T(8,128)}, f32[4,136,128]{2,1,0:T(8,128)}, f32[4,136,128]{2,1,0:T(8,128)}) custom-call(s32[4,16]{1,0:T(4,128)} %copy.13.pick_ref, s32[1]{0:T(128)} %bitcast.7.at_ref, f32[8,136,128]{2,1,0:T(8,128)} %copy-done.7, f32[8,136,128]{2,1,0:T(8,128)} %collective-permute-done.4.refs_1_), custom_call_target="tpu_custom_call" | custom-call | bytes 8388608 | tf_op jit(solution)/shard_map/pick/pallas_call | solution.py:108
  44.7 2.5 %collective-permute-start.8 = (f32[4,136,128]{2,1,0:T(8,128)}, f32[4,136,128]{2,1,0:T(8,128)S(1)}, u32[]{:S(2)}, u32[]{:S(2)}) collective-permute-start(f32[4,136,128]{2,1,0:T(8,128)} %get-tuple-element.21), channel_id=1, source_target_pairs={{0,24},{8,0},{16,8},{24,16},{1,25},{9,1},{17,9},{25,17},{2,26},{10... | collective-permute-start | bytes 835592 | tf_op jit(solution)/shard_map/ppermute | solution.py:387
  47.1 3.5 %collective-permute-done.5.refs_1_ = f32[8,136,128]{2,1,0:T(8,128)S(1)} collective-permute-done((f32[8,136,128]{2,1,0:T(8,128)}, f32[8,136,128]{2,1,0:T(8,128)S(1)}, u32[]{:S(2)}, u32[]{:S(2)}) %collective-permute-start.5) | collective-permute-done | bytes 557088 | tf_op jit(solution)/shard_map/ppermute | solution.py:360
  50.7 3.4 %collective-permute-start.7 = (f32[4,136,128]{2,1,0:T(8,128)S(1)}, f32[4,136,128]{2,1,0:T(8,128)S(1)}, u32[]{:S(2)}, u32[]{:S(2)}) collective-permute-start(f32[4,136,128]{2,1,0:T(8,128)S(1)} %slice.9), channel_id=1, source_target_pairs={{0,7},{1,0},{2,1},{3,2},{4,3},{5,4},{6,5},{7,6},{8,15},{9,8},{10,9... | collective-permute-start | bytes 835592 | tf_op jit(solution)/shard_map/ppermute | solution.py:360
  54.1 0.0 collective-permute-done.2.refs_0_
  54.1 0.1 collective-permute-start.6
  54.2 0.7 convert_reduce_fusion.1
  54.9 0.6 add_select_fusion.8
  55.5 1.0 collective-permute-start.12
  56.5 2.4 %collective-permute-start.13 = (f32[4,136,128]{2,1,0:T(8,128)}, f32[4,136,128]{2,1,0:T(8,128)S(1)}, u32[]{:S(2)}, u32[]{:S(2)}) collective-permute-start(f32[4,136,128]{2,1,0:T(8,128)} %get-tuple-element.29), channel_id=1, source_target_pairs={{0,16},{8,24},{16,0},{24,8},{1,17},{9,25},{17,1},{25,9},{2,18},{10... | collective-permute-start | bytes 835592 | tf_op jit(solution)/shard_map/ppermute | solution.py:387
  58.9 0.8 collective-permute-done.8.refs_4_
  59.7 0.0 collective-permute-done.7.refs_3_
  59.7 1.2 collective-permute-done.6.refs_2_
  60.9 3.3 %pick.4 = (f32[6,136,128]{2,1,0:T(8,128)}, f32[6,136,128]{2,1,0:T(8,128)}, f32[6,136,128]{2,1,0:T(8,128)}, f32[6,136,128]{2,1,0:T(8,128)}) custom-call(s32[4,16]{1,0:T(4,128)} %copy.13.pick_ref, s32[1]{0:T(128)} %bitcast.7.at_ref, f32[8,136,128]{2,1,0:T(8,128)} %copy-done.3, f32[8,136,128]{2,1,0:T(8,128)} %copy-done.2, ...), custom_call_target="tpu_custom_call" | custom-call | bytes 8388608 | tf_op jit(solution)/shard_map/pick/pallas_call | solution.py:108
  64.2 3.2 %collective-permute-start.9 = (f32[6,136,128]{2,1,0:T(8,128)}, f32[6,136,128]{2,1,0:T(8,128)S(1)}, u32[]{:S(2)}, u32[]{:S(2)}) collective-permute-start(f32[6,136,128]{2,1,0:T(8,128)} %get-tuple-element.23), channel_id=1, source_target_pairs={{0,8},{8,16},{16,24},{24,0},{1,9},{9,17},{17,25},{25,1},{2,10},{10... | collective-permute-start | bytes 1253384 | tf_op jit(solution)/shard_map/ppermute | solution.py:387
  67.4 1.5 %collective-permute-start.10 = (f32[6,136,128]{2,1,0:T(8,128)}, f32[6,136,128]{2,1,0:T(8,128)S(1)}, u32[]{:S(2)}, u32[]{:S(2)}) collective-permute-start(f32[6,136,128]{2,1,0:T(8,128)} %get-tuple-element.24), channel_id=1, source_target_pairs={{0,16},{8,24},{16,0},{24,8},{1,17},{9,25},{17,1},{25,9},{2,18},{10... | collective-permute-start | bytes 1253384 | tf_op jit(solution)/shard_map/ppermute | solution.py:387
  68.9 1.0 collective-permute-start.11
  69.9 1.2 compare_select_fusion.6
  71.1 0.1 select_reduce_fusion.4
  71.2 0.6 pad_add_fusion.1.slot_ref
  71.8 0.0 collective-permute-done.12.refs_2_
  71.8 0.0 collective-permute-done.13.refs_3_
  71.8 0.7 copy-done.12
  72.5 0.1 copy-done.13
  72.6 0.6 copy-done
  73.2 8.7 %terms.2 = (f32[64,128,128]{2,1,0:T(8,128)}, s32[264]{0:T(512)}) custom-call(s32[4,64]{1,0:T(4,128)} %pad_add_fusion.1.slot_ref, bf16[64,256,128]{2,1,0:T(8,128)(2,1)} %bitcast.10, f32[24,136,128]{2,1,0:T(8,128)} %bitcast.12, f32[4,136,128]{2,1,0:T(8,128)} %get-tuple-element.27.refs_1_, f32[4,136,128]{2,1,0:T(8,128)} %copy-done.12, ...), custom_call_target="tpu_custom_call" | custom-call | flops 1073741824 | bytes 16777216 | tf_op jit(solution)/shard_map/terms/pallas_call | solution.py:247
  81.9 5.9 %collective-permute-done.10.refs_2_ = f32[6,136,128]{2,1,0:T(8,128)S(1)} collective-permute-done((f32[6,136,128]{2,1,0:T(8,128)}, f32[6,136,128]{2,1,0:T(8,128)S(1)}, u32[]{:S(2)}, u32[]{:S(2)}) %collective-permute-start.10) | collective-permute-done | bytes 417824 | tf_op jit(solution)/shard_map/ppermute | solution.py:387
  87.9 0.0 collective-permute-done.11.refs_3_
  87.9 0.7 copy-done.10
  88.6 0.2 copy-done.11
  88.8 7.0 %terms.3 = (f32[64,128,128]{2,1,0:T(8,128)}, s32[264]{0:T(512)}, f32[256,1,128]{2,1,0:T(1,128)}) custom-call(s32[4,64]{1,0:T(4,128)} %pad_add_fusion.1.slot_ref, bf16[64,256,128]{2,1,0:T(8,128)(2,1)} %bitcast.11, f32[6,136,128]{2,1,0:T(8,128)} %get-tuple-element.22.refs_0_, f32[6,136,128]{2,1,0:T(8,128)} %copy-done.9, f32[6,136,128]{2,1,0:T(8,128)} %copy-done.10, ...), custom_call_target="tpu_custom_call" | custom-call | flops 1073741824 | bytes 16777216 | tf_op jit(solution)/shard_map/terms/pallas_call | solution.py:247
  95.7 10.5 %all-to-all-start.2 = ((f32[256,1,128]{2,1,0:T(1,128)}), f32[256,1,128]{2,1,0:T(1,128)S(1)}, u32[]{:S(2)}, u32[]{:S(2)}) async-start(f32[256,1,128]{2,1,0:T(1,128)} %get-tuple-element.33), calls=%async_computation.2 | async-start | bytes 262144 | tf_op jit(solution)/shard_map/all_to_all | solution.py:361
  106.2 4.4 %clear.1._ = f32[128,128,128]{2,1,0:T(8,128)} custom-call(s32[264]{0:T(512)} %get-tuple-element.32.used_ref), custom_call_target="tpu_custom_call" | custom-call | bytes 8388608 | tf_op jit(solution)/shard_map/clear/pallas_call | solution.py:293
  110.7 8.6 %all-to-all-done.2.most_ref = f32[256,1,128]{2,1,0:T(1,128)S(1)} async-done(((f32[256,1,128]{2,1,0:T(1,128)}), f32[256,1,128]{2,1,0:T(1,128)S(1)}, u32[]{:S(2)}, u32[]{:S(2)}) %all-to-all-start.2) | async-done | bytes 131104 | tf_op jit(solution)/shard_map/all_to_all | solution.py:361
  119.3 0.6 copy-done.8
  119.9 3.9 %scale.1 = f32[128,128,128]{2,1,0:T(8,128)} custom-call(s32[264]{0:T(512)} %get-tuple-element.32.used_ref, f32[256,1,128]{2,1,0:T(1,128)} %copy-done.8, f32[64,128,128]{2,1,0:T(8,128)} %get-tuple-element.34.tiles_ref, f32[128,128,128]{2,1,0:T(8,128)} %clear.1._), custom_call_target="tpu_custom_call", output_to_operand_aliasing={{}: (3, {})} | custom-call | tf_op jit(solution)/shard_map/scale/pallas_call | solution.py:327
  (40 shorter events, 0.2 us)
Async XLA Ops:
  1.9 26.1 %copy-start.1 = (f32[8,136,128]{2,1,0:T(8,128)}, f32[8,136,128]{2,1,0:T(8,128)S(1)}, u32[]{:S(2)}) copy-start(f32[8,136,128]{2,1,0:T(8,128)S(1)} %pad_maximum_fusion.refs_0_) | copy-start | bytes 1671172
  1.9 22.3 %collective-permute-start.3 = (f32[8,136,128]{2,1,0:T(8,128)S(1)}, f32[8,136,128]{2,1,0:T(8,128)S(1)}, u32[]{:S(2)}, u32[]{:S(2)}) collective-permute-start(f32[8,136,128]{2,1,0:T(8,128)S(1)} %pad_maximum_fusion.refs_0_), channel_id=1, source_target_pairs={{0,7},{1,0},{2,1},{3,2},{4,3},{5,4},{6,5},{7,6},{8,15},{9,8},{10,9... | collective-permute-start | bytes 1671176 | tf_op jit(solution)/shard_map/ppermute | solution.py:360
  8.4 18.6 %collective-permute-start = (f32[8,136,128]{2,1,0:T(8,128)S(1)}, f32[8,136,128]{2,1,0:T(8,128)S(1)}, u32[]{:S(2)}, u32[]{:S(2)}) collective-permute-start(f32[8,136,128]{2,1,0:T(8,128)S(1)} %pad_maximum_fusion.refs_0_), channel_id=1, source_target_pairs={{0,1},{1,2},{2,3},{3,4},{4,5},{5,6},{6,7},{7,0},{8,9},{9,10},{10,1... | collective-permute-start | bytes 1671176 | tf_op jit(solution)/shard_map/ppermute | solution.py:360
  11.8 15.2 %all-to-all-start = ((s32[4,8,8]{2,1,0:T(8,128)}), s32[4,8,8]{2,1,0:T(8,128)S(1)}, u32[]{:S(2)}, u32[]{:S(2)}) async-start(s32[4,8,8]{2,1,0:T(8,128)} %broadcast_in_dim.117), calls=%async_computation | async-start | bytes 32768 | tf_op jit(solution)/shard_map/all_to_all | solution.py:361
  24.2 3.8 %copy-start.6 = (f32[8,136,128]{2,1,0:T(8,128)}, f32[8,136,128]{2,1,0:T(8,128)S(1)}, u32[]{:S(2)}) copy-start(f32[8,136,128]{2,1,0:T(8,128)S(1)} %collective-permute-done.3.refs_2_) | copy-start | bytes 1671172
  24.2 13.2 %collective-permute-start.4 = (f32[8,136,128]{2,1,0:T(8,128)S(1)}, f32[8,136,128]{2,1,0:T(8,128)}, u32[]{:S(2)}, u32[]{:S(2)}) collective-permute-start(f32[8,136,128]{2,1,0:T(8,128)S(1)} %collective-permute-done.3.refs_2_), channel_id=1, source_target_pairs={{0,7},{1,0},{2,1},{3,2},{4,3},{5,4},{6,5},{7,6},{8,15},{9,8},{10,9... | collective-permute-start | bytes 1671176 | tf_op jit(solution)/shard_map/ppermute | solution.py:360
  27.0 1.0 copy-start.5
  27.0 13.9 %collective-permute-start.1 = (f32[8,136,128]{2,1,0:T(8,128)S(1)}, f32[8,136,128]{2,1,0:T(8,128)S(1)}, u32[]{:S(2)}, u32[]{:S(2)}) collective-permute-start(f32[8,136,128]{2,1,0:T(8,128)S(1)} %collective-permute-done.refs_1_), channel_id=1, source_target_pairs={{0,1},{1,2},{2,3},{3,4},{4,5},{5,6},{6,7},{7,0},{8,9},{9,10},{10,1... | collective-permute-start | bytes 1671176 | tf_op jit(solution)/shard_map/ppermute | solution.py:360
  28.0 26.2 %copy-start.15 = (s32[8]{0:T(128)S(1)}, s32[8]{0:T(128)}, u32[]{:S(2)}) copy-start(s32[8]{0:T(128)} %param.7) | copy-start | bytes 100
  31.5 40.3 %all-to-all-start.1 = ((f32[4,6,136,128]{3,2,1,0:T(8,128)}), f32[4,6,136,128]{3,2,1,0:T(8,128)S(1)}, u32[]{:S(2)}, u32[]{:S(2)}) async-start(f32[4,6,136,128]{3,2,1,0:T(8,128)} %pick.5), calls=%async_computation.1 | async-start | bytes 3342336 | tf_op jit(solution)/shard_map/all_to_all | solution.py:361
  37.4 13.3 %collective-permute-start.5 = (f32[8,136,128]{2,1,0:T(8,128)}, f32[8,136,128]{2,1,0:T(8,128)S(1)}, u32[]{:S(2)}, u32[]{:S(2)}) collective-permute-start(f32[8,136,128]{2,1,0:T(8,128)} %collective-permute-done.4.refs_1_), channel_id=1, source_target_pairs={{0,7},{1,0},{2,1},{3,2},{4,3},{5,4},{6,5},{7,6},{8,15},{9,8},{10,9... | collective-permute-start | bytes 1671176 | tf_op jit(solution)/shard_map/ppermute | solution.py:360
  40.9 0.8 copy-start.7
  40.9 13.2 %collective-permute-start.2 = (f32[8,136,128]{2,1,0:T(8,128)S(1)}, f32[8,136,128]{2,1,0:T(8,128)S(1)}, u32[]{:S(2)}, u32[]{:S(2)}) collective-permute-start(f32[8,136,128]{2,1,0:T(8,128)S(1)} %collective-permute-done.1.refs_0_), channel_id=1, source_target_pairs={{0,1},{1,2},{2,3},{3,4},{4,5},{5,6},{6,7},{7,0},{8,9},{9,10},{10,1... | collective-permute-start | bytes 1671176 | tf_op jit(solution)/shard_map/ppermute | solution.py:360
  44.7 15.1 %collective-permute-start.8 = (f32[4,136,128]{2,1,0:T(8,128)}, f32[4,136,128]{2,1,0:T(8,128)S(1)}, u32[]{:S(2)}, u32[]{:S(2)}) collective-permute-start(f32[4,136,128]{2,1,0:T(8,128)} %get-tuple-element.21), channel_id=1, source_target_pairs={{0,24},{8,0},{16,8},{24,16},{1,25},{9,1},{17,9},{25,17},{2,26},{10... | collective-permute-start | bytes 835592 | tf_op jit(solution)/shard_map/ppermute | solution.py:387
  50.7 10.2 %copy-start.2 = (f32[8,136,128]{2,1,0:T(8,128)}, f32[8,136,128]{2,1,0:T(8,128)S(1)}, u32[]{:S(2)}) copy-start(f32[8,136,128]{2,1,0:T(8,128)S(1)} %collective-permute-done.5.refs_1_) | copy-start | bytes 1671172
  50.7 9.0 %collective-permute-start.7 = (f32[4,136,128]{2,1,0:T(8,128)S(1)}, f32[4,136,128]{2,1,0:T(8,128)S(1)}, u32[]{:S(2)}, u32[]{:S(2)}) collective-permute-start(f32[4,136,128]{2,1,0:T(8,128)S(1)} %slice.9), channel_id=1, source_target_pairs={{0,7},{1,0},{2,1},{3,2},{4,3},{5,4},{6,5},{7,6},{8,15},{9,8},{10,9... | collective-permute-start | bytes 835592 | tf_op jit(solution)/shard_map/ppermute | solution.py:360
  54.1 6.8 %copy-start.3 = (f32[8,136,128]{2,1,0:T(8,128)}, f32[8,136,128]{2,1,0:T(8,128)S(1)}, u32[]{:S(2)}) copy-start(f32[8,136,128]{2,1,0:T(8,128)S(1)} %collective-permute-done.2.refs_0_) | copy-start | bytes 1671172
  54.1 6.8 %collective-permute-start.6 = (f32[4,136,128]{2,1,0:T(8,128)S(1)}, f32[4,136,128]{2,1,0:T(8,128)}, u32[]{:S(2)}, u32[]{:S(2)}) collective-permute-start(f32[4,136,128]{2,1,0:T(8,128)S(1)} %slice.8), channel_id=1, source_target_pairs={{0,1},{1,2},{2,3},{3,4},{4,5},{5,6},{6,7},{7,0},{8,9},{9,10},{10,1... | collective-permute-start | bytes 835592 | tf_op jit(solution)/shard_map/ppermute | solution.py:360
  55.5 16.3 %collective-permute-start.12 = (f32[4,136,128]{2,1,0:T(8,128)}, f32[4,136,128]{2,1,0:T(8,128)S(1)}, u32[]{:S(2)}, u32[]{:S(2)}) collective-permute-start(f32[4,136,128]{2,1,0:T(8,128)} %get-tuple-element.28), channel_id=1, source_target_pairs={{0,8},{8,16},{16,24},{24,0},{1,9},{9,17},{17,25},{25,1},{2,10},{10... | collective-permute-start | bytes 835592 | tf_op jit(solution)/shard_map/ppermute | solution.py:387
  56.5 15.3 %collective-permute-start.13 = (f32[4,136,128]{2,1,0:T(8,128)}, f32[4,136,128]{2,1,0:T(8,128)S(1)}, u32[]{:S(2)}, u32[]{:S(2)}) collective-permute-start(f32[4,136,128]{2,1,0:T(8,128)} %get-tuple-element.29), channel_id=1, source_target_pairs={{0,16},{8,24},{16,0},{24,8},{1,17},{9,25},{17,1},{25,9},{2,18},{10... | collective-permute-start | bytes 835592 | tf_op jit(solution)/shard_map/ppermute | solution.py:387
  59.7 1.2 copy-start.4
  59.7 1.2 copy-start.14
  64.2 17.7 %collective-permute-start.9 = (f32[6,136,128]{2,1,0:T(8,128)}, f32[6,136,128]{2,1,0:T(8,128)S(1)}, u32[]{:S(2)}, u32[]{:S(2)}) collective-permute-start(f32[6,136,128]{2,1,0:T(8,128)} %get-tuple-element.23), channel_id=1, source_target_pairs={{0,8},{8,16},{16,24},{24,0},{1,9},{9,17},{17,25},{25,1},{2,10},{10... | collective-permute-start | bytes 1253384 | tf_op jit(solution)/shard_map/ppermute | solution.py:387
  67.4 20.4 %collective-permute-start.10 = (f32[6,136,128]{2,1,0:T(8,128)}, f32[6,136,128]{2,1,0:T(8,128)S(1)}, u32[]{:S(2)}, u32[]{:S(2)}) collective-permute-start(f32[6,136,128]{2,1,0:T(8,128)} %get-tuple-element.24), channel_id=1, source_target_pairs={{0,16},{8,24},{16,0},{24,8},{1,17},{9,25},{17,1},{25,9},{2,18},{10... | collective-permute-start | bytes 1253384 | tf_op jit(solution)/shard_map/ppermute | solution.py:387
  68.9 18.9 %collective-permute-start.11 = (f32[6,136,128]{2,1,0:T(8,128)}, f32[6,136,128]{2,1,0:T(8,128)S(1)}, u32[]{:S(2)}, u32[]{:S(2)}) collective-permute-start(f32[6,136,128]{2,1,0:T(8,128)} %get-tuple-element.25), channel_id=1, source_target_pairs={{0,24},{8,0},{16,8},{24,16},{1,25},{9,1},{17,9},{25,17},{2,26},{10... | collective-permute-start | bytes 1253384 | tf_op jit(solution)/shard_map/ppermute | solution.py:387
  71.8 0.7 copy-start.12
  71.8 0.8 copy-start.13
  71.8 1.4 %copy-start = (f32[4,6,136,128]{3,2,1,0:T(8,128)}, f32[4,6,136,128]{3,2,1,0:T(8,128)S(1)}, u32[]{:S(2)}) copy-start(f32[4,6,136,128]{3,2,1,0:T(8,128)S(1)} %all-to-all-done.1) | copy-start | bytes 5013508
  81.9 5.9 %copy-start.9 = (f32[6,136,128]{2,1,0:T(8,128)}, f32[6,136,128]{2,1,0:T(8,128)S(1)}, u32[]{:S(2)}) copy-start(f32[6,136,128]{2,1,0:T(8,128)S(1)} %collective-permute-done.9.refs_1_) | copy-start | bytes 1253380
  87.8 0.8 copy-start.10
  87.9 0.9 copy-start.11
  95.7 23.5 %all-to-all-start.2 = ((f32[256,1,128]{2,1,0:T(1,128)}), f32[256,1,128]{2,1,0:T(1,128)S(1)}, u32[]{:S(2)}, u32[]{:S(2)}) async-start(f32[256,1,128]{2,1,0:T(1,128)} %get-tuple-element.33), calls=%async_computation.2 | async-start | bytes 262144 | tf_op jit(solution)/shard_map/all_to_all | solution.py:361
  119.3 0.6 copy-start.8

commit v4 on v3

--- a/solution.py
+++ b/solution.py
@@ -17,7 +17,7 @@
 VMEM = pl.BlockSpec(memory_space=pltpu.VMEM)
 HBM = pl.BlockSpec(memory_space=pltpu.HBM)
 MIB = 1 << 20
-UNROLL = 4
+UNROLL = 8
 CHUNK = 8
 CUTS = (1,2)
 MERGED = 1
@@ -31,9 +31,10 @@
 
 
 def dot_split(left, right):
-    n = right.shape[0]
-    four = jnp.dot(left, right, preferred_element_type=jnp.float32)
-    return four[:n, :n] + ((four[:n, n:] + four[n:, :n]) + four[n:, n:])
+    n = left.shape[0]
+    left = jnp.concatenate([left, left[:, :n]], axis=1)
+    right = jnp.concatenate([right[:n], right], axis=0)
+    return jnp.dot(left, right, preferred_element_type=jnp.float32)
 
 
 def params(mib):
@@ -41,9 +42,9 @@
 
 
 def inner_kernel(blocks_ref, prolong_ref, out_ref, done_ref):
-    left = split(prolong_ref[0].T, 0)
+    left = split(prolong_ref[0].T, 1)
     for k in range(blocks_ref.shape[1]):
-        out_ref[0, k] = split(dot_split(left, split(blocks_ref[0, k], 1)), 0)
+        out_ref[0, k] = split(dot_split(left, split(blocks_ref[0, k], 0)), 1)
     done_ref[...] = jnp.zeros_like(done_ref)
 
 
@@ -57,11 +58,11 @@
             pl.BlockSpec((1, tile, tile), lambda i: (i, 0, 0)),
         ],
         out_specs=[
-            pl.BlockSpec((1, slots, 2 * tile, tile), lambda i: (i, 0, 0, 0)),
+            pl.BlockSpec((1, slots, tile, 2 * tile), lambda i: (i, 0, 0, 0)),
             pl.BlockSpec((8, tile), lambda i: (0, 0)),
         ],
         out_shape=[
-            pltpu.HBM((rows, slots, 2 * tile, tile), jnp.bfloat16),
+            pltpu.HBM((rows, slots, tile, 2 * tile), jnp.bfloat16),
             jax.ShapeDtypeStruct((8, tile), jnp.float32),
         ],
         cost_estimate=pl.CostEstimate(
@@ -177,7 +178,7 @@
     look_up = pltpu.make_async_copy(ids, agg_ref, sem)
     look_up.start()
     for n in range(at):
-        right[n] = split(held[n, :tile], 1)
+        right[n] = split(held[n, :tile], 0)
     loads(lambda copy: copy.wait())
     look_up.wait()
     if final:
@@ -241,7 +242,7 @@
 
 
 def sum_terms(slots, inner, parts, first, wide, everyone, before=()):
-    flat, _, tile = inner.shape
+    flat, tile, _ = inner.shape
     final = len(before) > 0
     count = sum(p.shape[0] for p in parts)
     return pl.pallas_call(
@@ -256,7 +257,7 @@
         scratch_shapes=[
             pltpu.VMEM(inner.shape, jnp.bfloat16),
             pltpu.VMEM((count, *parts[0].shape[1:]), jnp.float32),
-            pltpu.VMEM((count, tile, 2 * tile), jnp.bfloat16),
+            pltpu.VMEM((count, 2 * tile, tile), jnp.bfloat16),
             pltpu.VMEM((flat + 1, tile, tile), jnp.float32),
             pltpu.VMEM((AGD, tile, tile), jnp.float32),
             pltpu.VMEM((count, tile), jnp.int32),
@@ -366,7 +367,7 @@
     note = jnp.where(live, columns, -1)
     theirs = swap(jnp.broadcast_to(note, (ny, *note.shape)))
     inner, done = inner_products(blocks, prolong)
-    inner = inner.reshape(flat, 2 * tile, tile)
+    inner = inner.reshape(flat, tile, 2 * tile)
     apart = jnp.arange(nz, dtype=jnp.int32)
     owners = my_y * nz + (my_z + apart) % nz
     low, high = wanted_ends(theirs, owners, rows)

time: 125 us -> 124 us (level)
  Pallas kernels: 42 us -> 39.6 us
  waiting for transfers between devices: 21.7 us -> 23.3 us
    pallas_call x2, Pallas kernels: 15.7 us -> 13.6 us  [sum_terms(): pl.pallas_call(functools.partial(terms_kernel, first, final, len(parts)),...]
    ppermute x6, waiting for transfers between devices: 6.77 us -> 8.44 us  [per_device(): lax.ppermute(x, 'col_0', [(i, (i + d) % ny) for i in range(ny)])]
  transfers between devices with their start and end apart: 17 -> 17, of which waited for: 6 -> 6; matrix products, arithmetic and copies ran while one was open for 6% -> 6% of each run, Pallas kernels for 25% -> 24%
where the time goes in v4:
time: 124 us; the launch traced here: 123 us
  starting transfers between devices  46.8 us (38%)
  Pallas kernels  39.6 us (32%)
  waiting for transfers between devices  23.3 us (19%)
  other arithmetic  7.08 us (6%)
  local copies, waits for them, and re-layouts  6.14 us (5%)
    all_to_all x3, starting transfers between devices, per_device(): lax.all_to_all(x, axis, split_axis=0, concat_axis=0, tiled=True)  19.1 us
    ppermute x8, starting transfers between devices, per_device(): hop = lambda x, way: lax.ppermute(x, 'col_1', around[way])  16.2 us
    pallas_call x2, Pallas kernels, sum_terms(): pl.pallas_call(functools.partial(terms_kernel, first, final, len(parts)),...  13.6 us
    ppermute x6, starting transfers between devices, per_device(): lax.ppermute(x, 'col_0', [(i, (i + d) % ny) for i in range(ny)])  11.5 us
    pallas_call x3, Pallas kernels, pick(): pl.pallas_call(functools.partial(pick_kernel, steps, apart), in_specs=[SM...  9.73 us
    all_to_all x3, waiting for transfers between devices, per_device(): lax.all_to_all(x, axis, split_axis=0, concat_axis=0, tiled=True)  8.46 us
    ppermute x6, waiting for transfers between devices, per_device(): lax.ppermute(x, 'col_0', [(i, (i + d) % ny) for i in range(ny)])  8.44 us
    pallas_call x1, Pallas kernels, inner_products(): pl.pallas_call(inner_kernel, grid=(rows,), in_specs=[pl.BlockSpec((1, slo...  8.03 us
  transfers between devices with their start and end apart: 17, of which 6 were waited for; matrix products, arithmetic and copies ran while one was open for 6% of the time, Pallas kernels for 24%

profile of v4, /device:TPU:1, one launch (start us, length us, event | category | flops | bytes accessed | tf_op | source)
XLA Modules:
  0.0 123.4 jit_solution(7492915488097264714)
XLA Ops:
  0.0 0.7 fusion.27
  0.7 0.1 broadcast_in_dim.122
  0.8 1.1 pad_maximum_fusion.refs_0_
  1.9 6.5 %collective-permute-start.3 = (f32[8,136,128]{2,1,0:T(8,128)S(1)}, f32[8,136,128]{2,1,0:T(8,128)S(1)}, u32[]{:S(2)}, u32[]{:S(2)}) collective-permute-start(f32[8,136,128]{2,1,0:T(8,128)S(1)} %pad_maximum_fusion.refs_0_), channel_id=1, source_target_pairs={{0,7},{1,0},{2,1},{3,2},{4,3},{5,4},{6,5},{7,6},{8,15},{9,8},{10,9... | collective-permute-start | bytes 1671176 | tf_op jit(solution)/shard_map/ppermute | solution.py:361
  8.4 0.8 reshape.737
  9.2 0.1 broadcast_in_dim.112
  9.2 0.1 mul.349
  9.3 0.7 iota_compare_fusion.2
  10.1 0.1 lt.132
  10.1 0.2 select_reduce_fusion.7
  10.3 0.1 reduce_min.21
  10.4 0.8 fusion.21
  11.2 0.6 broadcast_in_dim.117
  11.8 4.2 %all-to-all-start = ((s32[4,8,8]{2,1,0:T(8,128)}), s32[4,8,8]{2,1,0:T(8,128)S(1)}, u32[]{:S(2)}, u32[]{:S(2)}) async-start(s32[4,8,8]{2,1,0:T(8,128)} %broadcast_in_dim.117), calls=%async_computation | async-start | bytes 32768 | tf_op jit(solution)/shard_map/all_to_all | solution.py:362
  16.0 8.0 %inner.1 = (bf16[8,8,128,256]{3,2,1,0:T(8,128)(2,1)}, f32[8,128]{1,0:T(8,128)}) custom-call(f32[8,8,128,128]{3,2,1,0:T(8,128)} %blocks_ref.1, f32[8,128,128]{2,1,0:T(8,128)} %prolong_ref.1), custom_call_target="tpu_custom_call" | custom-call | flops 1073741824 | bytes 9437184 | tf_op jit(solution)/shard_map/inner/pallas_call | solution.py:53
  24.0 0.0 collective-permute-done.3.refs_2_
  24.0 2.8 %collective-permute-start.4 = (f32[8,136,128]{2,1,0:T(8,128)S(1)}, f32[8,136,128]{2,1,0:T(8,128)}, u32[]{:S(2)}, u32[]{:S(2)}) collective-permute-start(f32[8,136,128]{2,1,0:T(8,128)S(1)} %collective-permute-done.3.refs_2_), channel_id=1, source_target_pairs={{0,7},{1,0},{2,1},{3,2},{4,3},{5,4},{6,5},{7,6},{8,15},{9,8},{10,9... | collective-permute-start | bytes 1671176 | tf_op jit(solution)/shard_map/ppermute | solution.py:361
  26.8 0.0 collective-permute-done.refs_1_
  26.8 0.0 collective-permute-start.1
  26.8 0.2 select_reduce_fusion.1
  27.0 0.1 copy.11
  27.1 0.7 copy.13.pick_ref
  27.8 3.5 %pick.5 = f32[4,6,136,128]{3,2,1,0:T(8,128)} custom-call(s32[4,16]{1,0:T(4,128)} %copy.13.pick_ref, s32[1]{0:T(128)} %bitcast.7.at_ref, f32[8,136,128]{2,1,0:T(8,128)} %copy-done.1, f32[8,136,128]{2,1,0:T(8,128)} %copy-done.5, f32[8,136,128]{2,1,0:T(8,128)} %copy-done.6, f32[8,128]{1,0:T(8,128)} %get-tuple-element.26.refs_3_), custom_call_target="tpu_custom_call" | custom-call | bytes 8388608 | tf_op jit(solution)/shard_map/pick/pallas_call | solution.py:109
  31.3 4.2 %all-to-all-start.1 = ((f32[4,6,136,128]{3,2,1,0:T(8,128)}), f32[4,6,136,128]{3,2,1,0:T(8,128)S(1)}, u32[]{:S(2)}, u32[]{:S(2)}) async-start(f32[4,6,136,128]{3,2,1,0:T(8,128)} %pick.5), calls=%async_computation.1 | async-start | bytes 3342336 | tf_op jit(solution)/shard_map/all_to_all | solution.py:362
  35.5 1.6 %collective-permute-done.4.refs_1_ = f32[8,136,128]{2,1,0:T(8,128)} collective-permute-done((f32[8,136,128]{2,1,0:T(8,128)S(1)}, f32[8,136,128]{2,1,0:T(8,128)}, u32[]{:S(2)}, u32[]{:S(2)}) %collective-permute-start.4) | collective-permute-done | bytes 557088 | tf_op jit(solution)/shard_map/ppermute | solution.py:361
  37.2 3.5 %collective-permute-start.5 = (f32[8,136,128]{2,1,0:T(8,128)}, f32[8,136,128]{2,1,0:T(8,128)S(1)}, u32[]{:S(2)}, u32[]{:S(2)}) collective-permute-start(f32[8,136,128]{2,1,0:T(8,128)} %collective-permute-done.4.refs_1_), channel_id=1, source_target_pairs={{0,7},{1,0},{2,1},{3,2},{4,3},{5,4},{6,5},{7,6},{8,15},{9,8},{10,9... | collective-permute-start | bytes 1671176 | tf_op jit(solution)/shard_map/ppermute | solution.py:361
  40.7 0.0 collective-permute-done.1.refs_0_
  40.7 0.0 collective-permute-start.2
  40.7 0.1 select_reduce_fusion.5
  40.9 0.7 copy-done.7
  41.5 2.9 %pick.3 = (f32[4,136,128]{2,1,0:T(8,128)}, f32[4,136,128]{2,1,0:T(8,128)}, f32[4,136,128]{2,1,0:T(8,128)}, f32[4,136,128]{2,1,0:T(8,128)}) custom-call(s32[4,16]{1,0:T(4,128)} %copy.13.pick_ref, s32[1]{0:T(128)} %bitcast.7.at_ref, f32[8,136,128]{2,1,0:T(8,128)} %copy-done.7, f32[8,136,128]{2,1,0:T(8,128)} %collective-permute-done.4.refs_1_), custom_call_target="tpu_custom_call" | custom-call | bytes 8388608 | tf_op jit(solution)/shard_map/pick/pallas_call | solution.py:109
  44.5 2.5 %collective-permute-start.8 = (f32[4,136,128]{2,1,0:T(8,128)}, f32[4,136,128]{2,1,0:T(8,128)S(1)}, u32[]{:S(2)}, u32[]{:S(2)}) collective-permute-start(f32[4,136,128]{2,1,0:T(8,128)} %get-tuple-element.21), channel_id=1, source_target_pairs={{0,24},{8,0},{16,8},{24,16},{1,25},{9,1},{17,9},{25,17},{2,26},{10... | collective-permute-start | bytes 835592 | tf_op jit(solution)/shard_map/ppermute | solution.py:388
  46.9 3.6 %collective-permute-done.5.refs_1_ = f32[8,136,128]{2,1,0:T(8,128)S(1)} collective-permute-done((f32[8,136,128]{2,1,0:T(8,128)}, f32[8,136,128]{2,1,0:T(8,128)S(1)}, u32[]{:S(2)}, u32[]{:S(2)}) %collective-permute-start.5) | collective-permute-done | bytes 557088 | tf_op jit(solution)/shard_map/ppermute | solution.py:361
  50.5 3.4 %collective-permute-start.7 = (f32[4,136,128]{2,1,0:T(8,128)S(1)}, f32[4,136,128]{2,1,0:T(8,128)S(1)}, u32[]{:S(2)}, u32[]{:S(2)}) collective-permute-start(f32[4,136,128]{2,1,0:T(8,128)S(1)} %slice.9), channel_id=1, source_target_pairs={{0,7},{1,0},{2,1},{3,2},{4,3},{5,4},{6,5},{7,6},{8,15},{9,8},{10,9... | collective-permute-start | bytes 835592 | tf_op jit(solution)/shard_map/ppermute | solution.py:361
  53.9 0.0 collective-permute-done.2.refs_0_
  53.9 0.1 collective-permute-start.6
  54.0 0.7 convert_reduce_fusion.1
  54.7 0.6 add_select_fusion.8
  55.3 1.0 collective-permute-start.12
  56.3 2.4 %collective-permute-start.13 = (f32[4,136,128]{2,1,0:T(8,128)}, f32[4,136,128]{2,1,0:T(8,128)S(1)}, u32[]{:S(2)}, u32[]{:S(2)}) collective-permute-start(f32[4,136,128]{2,1,0:T(8,128)} %get-tuple-element.29), channel_id=1, source_target_pairs={{0,16},{8,24},{16,0},{24,8},{1,17},{9,25},{17,1},{25,9},{2,18},{10... | collective-permute-start | bytes 835592 | tf_op jit(solution)/shard_map/ppermute | solution.py:388
  58.7 0.8 collective-permute-done.8.refs_4_
  59.5 1.2 collective-permute-done.6.refs_2_
  60.7 3.3 %pick.4 = (f32[6,136,128]{2,1,0:T(8,128)}, f32[6,136,128]{2,1,0:T(8,128)}, f32[6,136,128]{2,1,0:T(8,128)}, f32[6,136,128]{2,1,0:T(8,128)}) custom-call(s32[4,16]{1,0:T(4,128)} %copy.13.pick_ref, s32[1]{0:T(128)} %bitcast.7.at_ref, f32[8,136,128]{2,1,0:T(8,128)} %copy-done.3, f32[8,136,128]{2,1,0:T(8,128)} %copy-done.2, ...), custom_call_target="tpu_custom_call" | custom-call | bytes 8388608 | tf_op jit(solution)/shard_map/pick/pallas_call | solution.py:109
  64.1 3.1 %collective-permute-start.9 = (f32[6,136,128]{2,1,0:T(8,128)}, f32[6,136,128]{2,1,0:T(8,128)S(1)}, u32[]{:S(2)}, u32[]{:S(2)}) collective-permute-start(f32[6,136,128]{2,1,0:T(8,128)} %get-tuple-element.23), channel_id=1, source_target_pairs={{0,8},{8,16},{16,24},{24,0},{1,9},{9,17},{17,25},{25,1},{2,10},{10... | collective-permute-start | bytes 1253384 | tf_op jit(solution)/shard_map/ppermute | solution.py:388
  67.2 1.5 %collective-permute-start.10 = (f32[6,136,128]{2,1,0:T(8,128)}, f32[6,136,128]{2,1,0:T(8,128)S(1)}, u32[]{:S(2)}, u32[]{:S(2)}) collective-permute-start(f32[6,136,128]{2,1,0:T(8,128)} %get-tuple-element.24), channel_id=1, source_target_pairs={{0,16},{8,24},{16,0},{24,8},{1,17},{9,25},{17,1},{25,9},{2,18},{10... | collective-permute-start | bytes 1253384 | tf_op jit(solution)/shard_map/ppermute | solution.py:388
  68.7 1.0 collective-permute-start.11
  69.7 1.2 compare_select_fusion.6
  70.9 0.1 select_reduce_fusion.4
  71.0 0.6 pad_add_fusion.1.slot_ref
  71.6 0.0 collective-permute-done.12.refs_2_
  71.6 0.0 collective-permute-done.13.refs_3_
  71.7 0.7 copy-done.12
  72.3 0.1 copy-done.13
  72.4 0.6 copy-done
  73.0 7.0 %terms.2 = (f32[64,128,128]{2,1,0:T(8,128)}, s32[264]{0:T(512)}) custom-call(s32[4,64]{1,0:T(4,128)} %pad_add_fusion.1.slot_ref, bf16[64,128,256]{2,1,0:T(8,128)(2,1)} %bitcast.10, f32[24,136,128]{2,1,0:T(8,128)} %bitcast.12, f32[4,136,128]{2,1,0:T(8,128)} %get-tuple-element.27.refs_1_, f32[4,136,128]{2,1,0:T(8,128)} %copy-done.12, ...), custom_call_target="tpu_custom_call" | custom-call | flops 1073741824 | bytes 16777216 | tf_op jit(solution)/shard_map/terms/pallas_call | solution.py:248
  80.0 7.6 %collective-permute-done.10.refs_2_ = f32[6,136,128]{2,1,0:T(8,128)S(1)} collective-permute-done((f32[6,136,128]{2,1,0:T(8,128)}, f32[6,136,128]{2,1,0:T(8,128)S(1)}, u32[]{:S(2)}, u32[]{:S(2)}) %collective-permute-start.10) | collective-permute-done | bytes 417824 | tf_op jit(solution)/shard_map/ppermute | solution.py:388
  87.7 0.7 copy-done.10
  88.4 0.2 copy-done.11
  88.6 6.6 %terms.3 = (f32[64,128,128]{2,1,0:T(8,128)}, s32[264]{0:T(512)}, f32[256,1,128]{2,1,0:T(1,128)}) custom-call(s32[4,64]{1,0:T(4,128)} %pad_add_fusion.1.slot_ref, bf16[64,128,256]{2,1,0:T(8,128)(2,1)} %bitcast.11, f32[6,136,128]{2,1,0:T(8,128)} %get-tuple-element.22.refs_0_, f32[6,136,128]{2,1,0:T(8,128)} %copy-done.9, f32[6,136,128]{2,1,0:T(8,128)} %copy-done.10, ...), custom_call_target="tpu_custom_call" | custom-call | flops 1073741824 | bytes 16777216 | tf_op jit(solution)/shard_map/terms/pallas_call | solution.py:248
  95.1 10.7 %all-to-all-start.2 = ((f32[256,1,128]{2,1,0:T(1,128)}), f32[256,1,128]{2,1,0:T(1,128)S(1)}, u32[]{:S(2)}, u32[]{:S(2)}) async-start(f32[256,1,128]{2,1,0:T(1,128)} %get-tuple-element.33), calls=%async_computation.2 | async-start | bytes 262144 | tf_op jit(solution)/shard_map/all_to_all | solution.py:362
  105.8 4.6 %clear.1._ = f32[128,128,128]{2,1,0:T(8,128)} custom-call(s32[264]{0:T(512)} %get-tuple-element.32.used_ref), custom_call_target="tpu_custom_call" | custom-call | bytes 8388608 | tf_op jit(solution)/shard_map/clear/pallas_call | solution.py:294
  110.4 8.5 %all-to-all-done.2.most_ref = f32[256,1,128]{2,1,0:T(1,128)S(1)} async-done(((f32[256,1,128]{2,1,0:T(1,128)}), f32[256,1,128]{2,1,0:T(1,128)S(1)}, u32[]{:S(2)}, u32[]{:S(2)}) %all-to-all-start.2) | async-done | bytes 131104 | tf_op jit(solution)/shard_map/all_to_all | solution.py:362
  118.8 0.6 copy-done.8
  119.5 3.7 %scale.1 = f32[128,128,128]{2,1,0:T(8,128)} custom-call(s32[264]{0:T(512)} %get-tuple-element.32.used_ref, f32[256,1,128]{2,1,0:T(1,128)} %copy-done.8, f32[64,128,128]{2,1,0:T(8,128)} %get-tuple-element.34.tiles_ref, f32[128,128,128]{2,1,0:T(8,128)} %clear.1._), custom_call_target="tpu_custom_call", output_to_operand_aliasing={{}: (3, {})} | custom-call | tf_op jit(solution)/shard_map/scale/pallas_call | solution.py:328
  (40 shorter events, 0.2 us)
Async XLA Ops:
  1.9 25.9 %copy-start.1 = (f32[8,136,128]{2,1,0:T(8,128)}, f32[8,136,128]{2,1,0:T(8,128)S(1)}, u32[]{:S(2)}) copy-start(f32[8,136,128]{2,1,0:T(8,128)S(1)} %pad_maximum_fusion.refs_0_) | copy-start | bytes 1671172
  1.9 22.1 %collective-permute-start.3 = (f32[8,136,128]{2,1,0:T(8,128)S(1)}, f32[8,136,128]{2,1,0:T(8,128)S(1)}, u32[]{:S(2)}, u32[]{:S(2)}) collective-permute-start(f32[8,136,128]{2,1,0:T(8,128)S(1)} %pad_maximum_fusion.refs_0_), channel_id=1, source_target_pairs={{0,7},{1,0},{2,1},{3,2},{4,3},{5,4},{6,5},{7,6},{8,15},{9,8},{10,9... | collective-permute-start | bytes 1671176 | tf_op jit(solution)/shard_map/ppermute | solution.py:361
  8.4 18.4 %collective-permute-start = (f32[8,136,128]{2,1,0:T(8,128)S(1)}, f32[8,136,128]{2,1,0:T(8,128)S(1)}, u32[]{:S(2)}, u32[]{:S(2)}) collective-permute-start(f32[8,136,128]{2,1,0:T(8,128)S(1)} %pad_maximum_fusion.refs_0_), channel_id=1, source_target_pairs={{0,1},{1,2},{2,3},{3,4},{4,5},{5,6},{6,7},{7,0},{8,9},{9,10},{10,1... | collective-permute-start | bytes 1671176 | tf_op jit(solution)/shard_map/ppermute | solution.py:361
  11.8 15.0 %all-to-all-start = ((s32[4,8,8]{2,1,0:T(8,128)}), s32[4,8,8]{2,1,0:T(8,128)S(1)}, u32[]{:S(2)}, u32[]{:S(2)}) async-start(s32[4,8,8]{2,1,0:T(8,128)} %broadcast_in_dim.117), calls=%async_computation | async-start | bytes 32768 | tf_op jit(solution)/shard_map/all_to_all | solution.py:362
  24.0 3.8 %copy-start.6 = (f32[8,136,128]{2,1,0:T(8,128)}, f32[8,136,128]{2,1,0:T(8,128)S(1)}, u32[]{:S(2)}) copy-start(f32[8,136,128]{2,1,0:T(8,128)S(1)} %collective-permute-done.3.refs_2_) | copy-start | bytes 1671172
  24.0 13.2 %collective-permute-start.4 = (f32[8,136,128]{2,1,0:T(8,128)S(1)}, f32[8,136,128]{2,1,0:T(8,128)}, u32[]{:S(2)}, u32[]{:S(2)}) collective-permute-start(f32[8,136,128]{2,1,0:T(8,128)S(1)} %collective-permute-done.3.refs_2_), channel_id=1, source_target_pairs={{0,7},{1,0},{2,1},{3,2},{4,3},{5,4},{6,5},{7,6},{8,15},{9,8},{10,9... | collective-permute-start | bytes 1671176 | tf_op jit(solution)/shard_map/ppermute | solution.py:361
  26.8 1.0 copy-start.5
  26.8 13.9 %collective-permute-start.1 = (f32[8,136,128]{2,1,0:T(8,128)S(1)}, f32[8,136,128]{2,1,0:T(8,128)S(1)}, u32[]{:S(2)}, u32[]{:S(2)}) collective-permute-start(f32[8,136,128]{2,1,0:T(8,128)S(1)} %collective-permute-done.refs_1_), channel_id=1, source_target_pairs={{0,1},{1,2},{2,3},{3,4},{4,5},{5,6},{6,7},{7,0},{8,9},{9,10},{10,1... | collective-permute-start | bytes 1671176 | tf_op jit(solution)/shard_map/ppermute | solution.py:361
  27.8 26.2 %copy-start.15 = (s32[8]{0:T(128)S(1)}, s32[8]{0:T(128)}, u32[]{:S(2)}) copy-start(s32[8]{0:T(128)} %param.7) | copy-start | bytes 100
  31.3 40.3 %all-to-all-start.1 = ((f32[4,6,136,128]{3,2,1,0:T(8,128)}), f32[4,6,136,128]{3,2,1,0:T(8,128)S(1)}, u32[]{:S(2)}, u32[]{:S(2)}) async-start(f32[4,6,136,128]{3,2,1,0:T(8,128)} %pick.5), calls=%async_computation.1 | async-start | bytes 3342336 | tf_op jit(solution)/shard_map/all_to_all | solution.py:362
  37.2 13.3 %collective-permute-start.5 = (f32[8,136,128]{2,1,0:T(8,128)}, f32[8,136,128]{2,1,0:T(8,128)S(1)}, u32[]{:S(2)}, u32[]{:S(2)}) collective-permute-start(f32[8,136,128]{2,1,0:T(8,128)} %collective-permute-done.4.refs_1_), channel_id=1, source_target_pairs={{0,7},{1,0},{2,1},{3,2},{4,3},{5,4},{6,5},{7,6},{8,15},{9,8},{10,9... | collective-permute-start | bytes 1671176 | tf_op jit(solution)/shard_map/ppermute | solution.py:361
  40.7 0.8 copy-start.7
  40.7 13.2 %collective-permute-start.2 = (f32[8,136,128]{2,1,0:T(8,128)S(1)}, f32[8,136,128]{2,1,0:T(8,128)S(1)}, u32[]{:S(2)}, u32[]{:S(2)}) collective-permute-start(f32[8,136,128]{2,1,0:T(8,128)S(1)} %collective-permute-done.1.refs_0_), channel_id=1, source_target_pairs={{0,1},{1,2},{2,3},{3,4},{4,5},{5,6},{6,7},{7,0},{8,9},{9,10},{10,1... | collective-permute-start | bytes 1671176 | tf_op jit(solution)/shard_map/ppermute | solution.py:361
  44.5 15.0 %collective-permute-start.8 = (f32[4,136,128]{2,1,0:T(8,128)}, f32[4,136,128]{2,1,0:T(8,128)S(1)}, u32[]{:S(2)}, u32[]{:S(2)}) collective-permute-start(f32[4,136,128]{2,1,0:T(8,128)} %get-tuple-element.21), channel_id=1, source_target_pairs={{0,24},{8,0},{16,8},{24,16},{1,25},{9,1},{17,9},{25,17},{2,26},{10... | collective-permute-start | bytes 835592 | tf_op jit(solution)/shard_map/ppermute | solution.py:388
  50.5 10.2 %copy-start.2 = (f32[8,136,128]{2,1,0:T(8,128)}, f32[8,136,128]{2,1,0:T(8,128)S(1)}, u32[]{:S(2)}) copy-start(f32[8,136,128]{2,1,0:T(8,128)S(1)} %collective-permute-done.5.refs_1_) | copy-start | bytes 1671172
  50.5 9.0 %collective-permute-start.7 = (f32[4,136,128]{2,1,0:T(8,128)S(1)}, f32[4,136,128]{2,1,0:T(8,128)S(1)}, u32[]{:S(2)}, u32[]{:S(2)}) collective-permute-start(f32[4,136,128]{2,1,0:T(8,128)S(1)} %slice.9), channel_id=1, source_target_pairs={{0,7},{1,0},{2,1},{3,2},{4,3},{5,4},{6,5},{7,6},{8,15},{9,8},{10,9... | collective-permute-start | bytes 835592 | tf_op jit(solution)/shard_map/ppermute | solution.py:361
  53.9 6.8 %copy-start.3 = (f32[8,136,128]{2,1,0:T(8,128)}, f32[8,136,128]{2,1,0:T(8,128)S(1)}, u32[]{:S(2)}) copy-start(f32[8,136,128]{2,1,0:T(8,128)S(1)} %collective-permute-done.2.refs_0_) | copy-start | bytes 1671172
  53.9 6.8 %collective-permute-start.6 = (f32[4,136,128]{2,1,0:T(8,128)S(1)}, f32[4,136,128]{2,1,0:T(8,128)}, u32[]{:S(2)}, u32[]{:S(2)}) collective-permute-start(f32[4,136,128]{2,1,0:T(8,128)S(1)} %slice.8), channel_id=1, source_target_pairs={{0,1},{1,2},{2,3},{3,4},{4,5},{5,6},{6,7},{7,0},{8,9},{9,10},{10,1... | collective-permute-start | bytes 835592 | tf_op jit(solution)/shard_map/ppermute | solution.py:361
  55.3 16.3 %collective-permute-start.12 = (f32[4,136,128]{2,1,0:T(8,128)}, f32[4,136,128]{2,1,0:T(8,128)S(1)}, u32[]{:S(2)}, u32[]{:S(2)}) collective-permute-start(f32[4,136,128]{2,1,0:T(8,128)} %get-tuple-element.28), channel_id=1, source_target_pairs={{0,8},{8,16},{16,24},{24,0},{1,9},{9,17},{17,25},{25,1},{2,10},{10... | collective-permute-start | bytes 835592 | tf_op jit(solution)/shard_map/ppermute | solution.py:388
  56.3 15.3 %collective-permute-start.13 = (f32[4,136,128]{2,1,0:T(8,128)}, f32[4,136,128]{2,1,0:T(8,128)S(1)}, u32[]{:S(2)}, u32[]{:S(2)}) collective-permute-start(f32[4,136,128]{2,1,0:T(8,128)} %get-tuple-element.29), channel_id=1, source_target_pairs={{0,16},{8,24},{16,0},{24,8},{1,17},{9,25},{17,1},{25,9},{2,18},{10... | collective-permute-start | bytes 835592 | tf_op jit(solution)/shard_map/ppermute | solution.py:388
  59.5 1.2 %copy-start.4 = (f32[4,136,128]{2,1,0:T(8,128)}, f32[4,136,128]{2,1,0:T(8,128)S(1)}, u32[]{:S(2)}) copy-start(f32[4,136,128]{2,1,0:T(8,128)S(1)} %collective-permute-done.8.refs_4_) | copy-start | bytes 835588
  59.5 1.2 %copy-start.14 = (f32[4,136,128]{2,1,0:T(8,128)}, f32[4,136,128]{2,1,0:T(8,128)S(1)}, u32[]{:S(2)}) copy-start(f32[4,136,128]{2,1,0:T(8,128)S(1)} %collective-permute-done.7.refs_3_) | copy-start | bytes 835588
  64.1 16.0 %collective-permute-start.9 = (f32[6,136,128]{2,1,0:T(8,128)}, f32[6,136,128]{2,1,0:T(8,128)S(1)}, u32[]{:S(2)}, u32[]{:S(2)}) collective-permute-start(f32[6,136,128]{2,1,0:T(8,128)} %get-tuple-element.23), channel_id=1, source_target_pairs={{0,8},{8,16},{16,24},{24,0},{1,9},{9,17},{17,25},{25,1},{2,10},{10... | collective-permute-start | bytes 1253384 | tf_op jit(solution)/shard_map/ppermute | solution.py:388
  67.2 20.4 %collective-permute-start.10 = (f32[6,136,128]{2,1,0:T(8,128)}, f32[6,136,128]{2,1,0:T(8,128)S(1)}, u32[]{:S(2)}, u32[]{:S(2)}) collective-permute-start(f32[6,136,128]{2,1,0:T(8,128)} %get-tuple-element.24), channel_id=1, source_target_pairs={{0,16},{8,24},{16,0},{24,8},{1,17},{9,25},{17,1},{25,9},{2,18},{10... | collective-permute-start | bytes 1253384 | tf_op jit(solution)/shard_map/ppermute | solution.py:388
  68.7 18.9 %collective-permute-start.11 = (f32[6,136,128]{2,1,0:T(8,128)}, f32[6,136,128]{2,1,0:T(8,128)S(1)}, u32[]{:S(2)}, u32[]{:S(2)}) collective-permute-start(f32[6,136,128]{2,1,0:T(8,128)} %get-tuple-element.25), channel_id=1, source_target_pairs={{0,24},{8,0},{16,8},{24,16},{1,25},{9,1},{17,9},{25,17},{2,26},{10... | collective-permute-start | bytes 1253384 | tf_op jit(solution)/shard_map/ppermute | solution.py:388
  71.6 0.7 copy-start.12
  71.6 0.8 copy-start.13
  71.6 1.4 %copy-start = (f32[4,6,136,128]{3,2,1,0:T(8,128)}, f32[4,6,136,128]{3,2,1,0:T(8,128)S(1)}, u32[]{:S(2)}) copy-start(f32[4,6,136,128]{3,2,1,0:T(8,128)S(1)} %all-to-all-done.1) | copy-start | bytes 5013508
  80.0 7.6 %copy-start.9 = (f32[6,136,128]{2,1,0:T(8,128)}, f32[6,136,128]{2,1,0:T(8,128)S(1)}, u32[]{:S(2)}) copy-start(f32[6,136,128]{2,1,0:T(8,128)S(1)} %collective-permute-done.9.refs_1_) | copy-start | bytes 1253380
  87.7 0.8 copy-start.10
  87.7 0.9 copy-start.11
  95.1 23.7 %all-to-all-start.2 = ((f32[256,1,128]{2,1,0:T(1,128)}), f32[256,1,128]{2,1,0:T(1,128)S(1)}, u32[]{:S(2)}, u32[]{:S(2)}) async-start(f32[256,1,128]{2,1,0:T(1,128)} %get-tuple-element.33), calls=%async_computation.2 | async-start | bytes 262144 | tf_op jit(solution)/shard_map/all_to_all | solution.py:362
  118.8 0.6 copy-start.8
